TPU v7x, 512 devices: a whole 4x8x8 slice. The times are simulated.
512 devices in a mesh: group: 16 (over y, z_lo), brick: 32 (over x, z_hi, core).
Axes of the slice: x: 4, y: 8, z: 8 (z_hi: 4, z_lo: 2; z = z_hi * 2 + z_lo), core: 2. Of those that a mesh axis runs over, the one named last changes fastest.
Arguments:
- populations: float32 [19, 32, 128, 128], P(None, 'brick', 'group'), may hold values from 0.5 to 1.5
- membrane_rows: int32 [32, 128], P('brick'), may hold values from 60 to 67
- positions: float32 [16, 3, 16, 32, 128], P('group', None, None, 'brick'), may hold values from 0 to 1
- velocities: float32 [16, 3, 16, 32, 128], P('group', None, None, 'brick'), may hold values from -4 to 4
- kicks: float32 [16, 3, 16, 32, 128], P('group', None, None, 'brick'), may hold values from -5 to 5
- bead_types: int32 [16, 16, 32, 128], P('group', None, 'brick'), may hold values from 0 to 1
- bond_partner: int32 [16, 16, 32, 128], P('group', None, 'brick'), may hold values from 0 to 15, as said below
- tile_counts: int32 [16, 32, 128], P('group', 'brick'), may hold values from 4 to 16
Outputs:
- new_populations: float32 [19, 32, 128, 128], P(None, 'brick', 'group')
- cell_mean: float32 [3, 32, 128], P(None, 'brick')
- new_positions: float32 [16, 3, 16, 32, 128], P('group', None, None, 'brick')
- new_velocities: float32 [16, 3, 16, 32, 128], P('group', None, None, 'brick')
Inputs may be any that keep to these rules, and one draw needn't show every extreme that they name: bond_partner pairs slots of one tile: the partner of a slot's partner is the slot itself; a slot that is its own partner has no bond.
All inputs are finite; a program needn't handle non-finite values.
Results may differ from a plain program's by a relative error of at most 0.0003.
Values sent between devices are 32-bit elements; how exact they have to be, the bound alone decides.
A program may use at most 64 MiB of HBM per device.

v0:
```python
import math

import jax
import jax.numpy as jnp
import numpy as np
from jax import lax
from jax.sharding import PartitionSpec as P

VELOCITY_SET = np.array(
    [
        [0, 0, 0],
        [1, 0, 0],
        [-1, 0, 0],
        [0, 1, 0],
        [0, -1, 0],
        [0, 0, 1],
        [0, 0, -1],
        [1, 1, 0],
        [-1, -1, 0],
        [1, -1, 0],
        [-1, 1, 0],
        [1, 0, 1],
        [-1, 0, -1],
        [1, 0, -1],
        [-1, 0, 1],
        [0, 1, 1],
        [0, -1, -1],
        [0, 1, -1],
        [0, -1, 1],
    ],
    dtype=np.int32,
)
WEIGHT_SET = np.array([1.0 / 3.0] + [1.0 / 18.0] * 6 + [1.0 / 36.0] * 12)
OPPOSITE = (0, 2, 1, 4, 3, 6, 5, 8, 7, 10, 9, 12, 11, 14, 13, 16, 15, 18, 17)
FROM_BELOW = (3, 7, 10, 15, 17)
FROM_ABOVE = (4, 8, 9, 16, 18)
RELAX_TIME = 0.8
PUSH_VECTOR = (0.001, 0.0, 0.0)
COUPLE_RATE = 1.0
VELOCITY_SCALE = 0.1
DRAG_RATE = 5.0
REPEL_SAME = 25.0
REPEL_CROSS = 50.0
FRICTION = 4.5
NOISE_SCALE = 3.0 / math.sqrt(0.02)
TIME_STEP = 0.02
BOND_STIFF = 10.0
HALF_ROOT = 1.0 / math.sqrt(2.0)
HIGHEST = lax.Precision.HIGHEST


def extended(x, sides, width):
    for axis, dim in sides:
        devices, length = (lax.axis_size(axis), x.shape[dim])
        up = [(i, (i + 1) % devices) for i in range(devices)]
        down = [(j, i) for i, j in up]
        last = lax.slice_in_dim(x, length - width, length, axis=dim)
        leading = lax.slice_in_dim(x, 0, width, axis=dim)
        before = lax.ppermute(last, axis, up)
        after = lax.ppermute(leading, axis, down)
        x = jnp.concatenate([before, x, after], axis=dim)
    return x


def moments(lattice):
    weights = jnp.asarray(WEIGHT_SET, jnp.float32)
    carried = jnp.asarray(VELOCITY_SET * WEIGHT_SET[:, None], jnp.float32)
    density = jnp.einsum("q,qxyz->xyz", weights, lattice, precision=HIGHEST)
    flux = jnp.einsum("qc,qxyz->cxyz", carried, lattice, precision=HIGHEST)
    return (density, flux / density)


def collide(lattice, density, velocity, force):
    shifted = velocity + RELAX_TIME * force / density
    along = jnp.einsum(
        "qc,cxyz->qxyz", jnp.asarray(VELOCITY_SET, jnp.float32), shifted, precision=HIGHEST
    )
    square = jnp.sum(shifted * shifted, axis=0)
    equilibrium = density * (1.0 + 3.0 * along + 4.5 * along * along - 1.5 * square)
    return lattice - (lattice - equilibrium) / RELAX_TIME


def stream_local(padded, post, lattice_rows, total_rows):
    planes = post.shape[1]
    slab_rows = post.shape[2]
    moved_pops = []
    for number in range(19):
        shift_x = int(VELOCITY_SET[number][0])
        shift_y = int(VELOCITY_SET[number][1])
        shift_z = int(VELOCITY_SET[number][2])
        window = padded[
            number, 1 - shift_x : 1 - shift_x + planes, 1 - shift_y : 1 - shift_y + slab_rows, :
        ]
        rolled = jnp.roll(window, shift_z, axis=-1)
        if number in FROM_BELOW:
            rolled = jnp.where(lattice_rows == 0, post[OPPOSITE[number]], rolled)
        if number in FROM_ABOVE:
            rolled = jnp.where(lattice_rows == total_rows - 1, post[OPPOSITE[number]], rolled)
        moved_pops.append(rolled)
    return jnp.stack(moved_pops)


def lattice_step(lattice, density, velocity, force, lattice_rows, total_rows):
    post = collide(lattice, density, velocity, force)
    padded = extended(post, (("group", 2), ("brick", 1)), 1)
    return stream_local(padded, post, lattice_rows, total_rows)


def slab_pick(array, shift_x, shift_z):
    width = array.shape[-2] - 2
    return jnp.roll(array[..., 1 + shift_x : 1 + shift_x + width, :], -shift_z, axis=-1)


def bead_forces(
    places,
    speeds,
    kick_now,
    slot_state,
    far_places,
    far_speeds,
    far_kick,
    far_state,
    partner,
    occupied,
    drag_velocity,
    pick,
):
    capacity = places.shape[1]
    same_slot = jnp.eye(capacity, dtype=jnp.bool_)[:, :, None, None]
    totals = jnp.zeros_like(places)
    for shift_x in (-1, 0, 1):
        for shift_z in (-1, 0, 1):
            other_places = pick(far_places, shift_x, shift_z)
            other_speeds = pick(far_speeds, shift_x, shift_z)
            other_kick = pick(far_kick, shift_x, shift_z)
            other_state = pick(far_state, shift_x, shift_z)[None]
            offset = jnp.asarray([shift_x, 0.0, shift_z], jnp.float32).reshape(3, 1, 1, 1, 1)
            apart = places[:, :, None] - other_places[:, None] - offset
            dist_sq = jnp.sum(apart * apart, axis=0)
            weight = jnp.maximum(1.0 - dist_sq, 0.0)
            closing = jnp.sum(apart * (speeds[:, :, None] - other_speeds[:, None]), axis=0)
            own_state = slot_state[:, None]
            paired = (own_state < 2) & (other_state < 2)
            if shift_x == 0 and shift_z == 0:
                paired = paired & jnp.logical_not(same_slot)
            repel = jnp.where(own_state == other_state, REPEL_SAME, REPEL_CROSS)
            theta = (kick_now[:, None] + other_kick[None]) * HALF_ROOT
            strength = jnp.where(
                paired,
                repel * weight
                - FRICTION * weight * weight * closing
                + NOISE_SCALE * weight * theta,
                0.0,
            )
            totals = totals + jnp.sum(strength[None] * apart, axis=2)
    slot_ids = jnp.arange(capacity, dtype=jnp.int32)[:, None, None, None]
    match = partner[None] == slot_ids
    partner_places = jnp.sum(jnp.where(match[None], places[:, :, None], 0.0), axis=1)
    partner_alive = jnp.any(match & occupied[:, None], axis=0)
    bonded = occupied & partner_alive
    totals = totals + jnp.where(bonded[None], -BOND_STIFF * (places - partner_places), 0.0)
    totals = totals + DRAG_RATE * (drag_velocity[:, None] / VELOCITY_SCALE - speeds)
    return totals


def local(
    populations, membrane_rows, positions, velocities, kicks, bead_types, bond_partner, tile_counts
):
    slab_rows = populations.shape[2]
    total_rows = slab_rows * lax.axis_size("group")
    lattice_rows = (
        lax.axis_index("group") * slab_rows + jnp.arange(slab_rows, dtype=jnp.int32)[None, :, None]
    )
    onehot = lattice_rows == membrane_rows[:, None, :]
    density, velocity = moments(populations)
    owned = jnp.sum(jnp.where(onehot[None], velocity, 0.0), axis=2)
    drag_velocity = lax.psum(owned, "group")
    push_force = jnp.asarray(PUSH_VECTOR, jnp.float32)[:, None, None, None]
    first_step = lattice_step(populations, density, velocity, push_force, lattice_rows, total_rows)
    places = positions[0]
    speeds = velocities[0]
    capacity = places.shape[1]
    occupied = jnp.arange(capacity, dtype=jnp.int32)[:, None, None] < tile_counts[0][None]
    slot_state = jnp.where(occupied, bead_types[0], 2)
    far_state = extended(slot_state, (("brick", 1),), 1)
    partner = bond_partner[0]
    for step_number in range(kicks.shape[1]):
        kick_now = kicks[0, step_number]
        moving = extended(
            jnp.concatenate([places, speeds, kick_now[None]], axis=0), (("brick", 2),), 1
        )
        far_kick = moving[6]
        totals = bead_forces(
            places,
            speeds,
            kick_now,
            slot_state,
            moving[0:3],
            moving[3:6],
            far_kick,
            far_state,
            partner,
            occupied,
            drag_velocity,
            slab_pick,
        )
        speeds = jnp.where(occupied[None], speeds + TIME_STEP * totals, 0.0)
        places = places + TIME_STEP * speeds
    places = jnp.where(occupied[None], places, 0.0)
    speed_sum = jnp.sum(speeds, axis=1)
    count_value = tile_counts[0].astype(jnp.float32)
    pooled_sum, pooled_count = lax.psum((speed_sum, count_value), "group")
    cell_mean = pooled_sum / pooled_count
    density, velocity = moments(first_step)
    force = (
        jnp.where(
            onehot[None], COUPLE_RATE * (VELOCITY_SCALE * cell_mean[:, :, None, :] - velocity), 0.0
        )
        + push_force
    )
    second = lattice_step(first_step, density, velocity, force, lattice_rows, total_rows)
    return (second, cell_mean, places[None], speeds[None])


def solution(mesh):
    return jax.shard_map(
        local,
        mesh=mesh,
        in_specs=(
            P(None, "brick", "group", None),
            P("brick", None),
            P("group", None, None, "brick", None),
            P("group", None, None, "brick", None),
            P("group", None, None, "brick", None),
            P("group", None, "brick", None),
            P("group", None, "brick", None),
            P("group", "brick", None),
        ),
        out_specs=(
            P(None, "brick", "group", None),
            P(None, "brick", None),
            P("group", None, None, "brick", None),
            P("group", None, None, "brick", None),
        ),
        check_vma=False,
    )
```

profile of v0, /device:TPU:88, one launch (start us, length us, event | category | flops | bytes accessed | tf_op | source)
XLA Modules:
  0.0 185.0 jit_solution(10308925492833026658)
XLA Ops:
  0.7 0.7 slice_bitcast_fusion.21
  1.4 11.8 %collective-permute-start.6 = (f32[7,16,1,128]{3,1,0,2:T(8,128)S(1)}, f32[7,16,1,128]{3,1,0,2:T(8,128)S(1)}, u32[]{:S(2)}, u32[]{:S(2)}) collective-permute-start(f32[7,16,1,128]{3,1,0,2:T(8,128)S(1)} %pad_maximum_fusion.2), channel_id=1, source_target_pairs={{1,0},{2,1},{3,2},{4,3},{5,4},{6,5},{7,6},{8,7},{9,8},{10,9},{11,1... | collective-permute-start | bytes 172040 | tf_op jit(solution)/shard_map/ppermute | solution.py:60
  13.3 1.9 %collective-permute-start.5 = (f32[7,16,1,128]{3,1,0,2:T(8,128)S(1)}, f32[7,16,1,128]{3,1,0,2:T(8,128)S(1)}, u32[]{:S(2)}, u32[]{:S(2)}) collective-permute-start(f32[7,16,1,128]{3,1,0,2:T(8,128)S(1)} %pad_maximum_fusion.2), channel_id=1, source_target_pairs={{0,1},{1,2},{2,3},{3,4},{4,5},{5,6},{6,7},{7,8},{8,9},{9,10},{10,1... | collective-permute-start | bytes 172040 | tf_op jit(solution)/shard_map/ppermute | solution.py:59
  15.2 0.6 copy-done.13
  15.8 1.9 %collective-permute-start.4 = (s32[16,1,128]{2,0,1:T(8,128)S(1)}, s32[16,1,128]{2,0,1:T(8,128)S(1)}, u32[]{:S(2)}, u32[]{:S(2)}) collective-permute-start(s32[16,1,128]{2,0,1:T(8,128)S(1)} %fusion.163), channel_id=1, source_target_pairs={{0,1},{1,2},{2,3},{3,4},{4,5},{5,6},{6,7},{7,8},{8,9},{9,10},{10,1... | collective-permute-start | bytes 24584 | tf_op jit(solution)/shard_map/ppermute | solution.py:59
  17.8 7.9 %collective-permute-start.7 = (s32[16,1,128]{2,0,1:T(8,128)S(1)}, s32[16,1,128]{2,0,1:T(8,128)S(1)}, u32[]{:S(2)}, u32[]{:S(2)}) collective-permute-start(s32[16,1,128]{2,0,1:T(8,128)S(1)} %fusion.163), channel_id=1, source_target_pairs={{1,0},{2,1},{3,2},{4,3},{5,4},{6,5},{7,6},{8,7},{9,8},{10,9},{11,1... | collective-permute-start | bytes 24584 | tf_op jit(solution)/shard_map/ppermute | solution.py:60
  25.7 0.6 copy-done.15
  26.3 0.2 fusion.99
  26.5 0.6 copy-done.16
  27.2 0.6 copy-done.18
  27.9 0.2 select_reduce_fusion.3
  28.1 0.7 copy-done.14
  28.7 0.3 fusion.175
  29.1 4.7 %collective-permute-start = (f32[19,1,1,128]{3,2,1,0:T(1,128)S(1)}, f32[19,1,1,128]{3,2,1,0:T(1,128)S(1)}, u32[]{:S(2)}, u32[]{:S(2)}) collective-permute-start(f32[19,1,1,128]{3,2,1,0:T(1,128)S(1)} %get-tuple-element.211), channel_id=1, source_target_pairs={{0,32},{32,64},{64,96},{96,128},{128,160},{160,192},{192,224},{224... | collective-permute-start | bytes 29192 | tf_op jit(solution)/shard_map/ppermute | solution.py:59
  34.4 0.7 copy-done.4
  35.1 30.4 %psum.21 = f32[3,1,128]{2,0,1:T(4,128)S(1)} all-reduce(f32[3,1,128]{2,0,1:T(4,128)S(1)} %bitcast.653), channel_id=1, replica_groups=mesh['group'=16,'brick'=32] {'group'}, use_global_device_ids=true, to_apply=%region_31.32 | all-reduce | flops 384 | bytes 3072 | tf_op jit(solution)/shard_map/psum | solution.py:177
  65.7 3.0 %collective-permute-start.1 = (f32[19,1,1,128]{3,2,1,0:T(1,128)S(1)}, f32[19,1,1,128]{3,2,1,0:T(1,128)S(1)}, u32[]{:S(2)}, u32[]{:S(2)}) collective-permute-start(f32[19,1,1,128]{3,2,1,0:T(1,128)S(1)} %get-tuple-element.212), channel_id=1, source_target_pairs={{32,0},{64,32},{96,64},{128,96},{160,128},{192,160},{224,192},{256... | collective-permute-start | bytes 29192 | tf_op jit(solution)/shard_map/ppermute | solution.py:60
  69.4 4.3 %collective-permute-done.1 = f32[19,1,1,128]{3,2,1,0:T(1,128)S(1)} collective-permute-done((f32[19,1,1,128]{3,2,1,0:T(1,128)S(1)}, f32[19,1,1,128]{3,2,1,0:T(1,128)S(1)}, u32[]{:S(2)}, u32[]{:S(2)}) %collective-permute-start.1) | collective-permute-done | bytes 9760 | tf_op jit(solution)/shard_map/ppermute | solution.py:60
  73.7 1.9 %collective-permute-start.2 = (f32[19,1,10,128]{3,2,1,0:T(8,128)S(1)}, f32[19,1,10,128]{3,2,1,0:T(8,128)S(1)}, u32[]{:S(2)}, u32[]{:S(2)}) collective-permute-start(f32[19,1,10,128]{3,2,1,0:T(8,128)S(1)} %pad_maximum_fusion), channel_id=1, source_target_pairs={{0,1},{1,2},{2,3},{3,4},{4,5},{5,6},{6,7},{7,8},{8,9},{9,10},{10,1... | collective-permute-start | bytes 291848 | tf_op jit(solution)/shard_map/ppermute | solution.py:59
  75.6 7.9 %collective-permute-start.3 = (f32[19,1,10,128]{3,2,1,0:T(8,128)S(1)}, f32[19,1,10,128]{3,2,1,0:T(8,128)S(1)}, u32[]{:S(2)}, u32[]{:S(2)}) collective-permute-start(f32[19,1,10,128]{3,2,1,0:T(8,128)S(1)} %pad_maximum_fusion), channel_id=1, source_target_pairs={{1,0},{2,1},{3,2},{4,3},{5,4},{6,5},{7,6},{8,7},{9,8},{10,9},{11,1... | collective-permute-start | bytes 291848 | tf_op jit(solution)/shard_map/ppermute | solution.py:60
  84.7 0.6 copy-done.11
  85.4 0.6 multiply_reduce_fusion.50
  86.0 0.2 and_select_fusion.23
  86.3 0.6 copy-done.5
  86.9 0.6 multiply_reduce_fusion.53
  87.5 0.2 and_select_fusion.5
  87.7 0.2 and_select_fusion.11
  87.9 0.6 multiply_reduce_fusion.63
  88.6 0.2 fusion.25
  88.7 0.2 multiply_reduce_fusion.60
  89.0 1.9 %collective-permute-start.8 = (f32[7,16,1,128]{3,1,0,2:T(8,128)S(1)}, f32[7,16,1,128]{3,1,0,2:T(8,128)S(1)}, u32[]{:S(2)}, u32[]{:S(2)}) collective-permute-start(f32[7,16,1,128]{3,1,0,2:T(8,128)S(1)} %pad_maximum_fusion.3), channel_id=1, source_target_pairs={{0,1},{1,2},{2,3},{3,4},{4,5},{5,6},{6,7},{7,8},{8,9},{9,10},{10,1... | collective-permute-start | bytes 172040 | tf_op jit(solution)/shard_map/ppermute | solution.py:59
  91.0 7.9 %collective-permute-start.9 = (f32[7,16,1,128]{3,1,0,2:T(8,128)S(1)}, f32[7,16,1,128]{3,1,0,2:T(8,128)S(1)}, u32[]{:S(2)}, u32[]{:S(2)}) collective-permute-start(f32[7,16,1,128]{3,1,0,2:T(8,128)S(1)} %pad_maximum_fusion.3), channel_id=1, source_target_pairs={{1,0},{2,1},{3,2},{4,3},{5,4},{6,5},{7,6},{8,7},{9,8},{10,9},{11,1... | collective-permute-start | bytes 172040 | tf_op jit(solution)/shard_map/ppermute | solution.py:60
  101.4 0.2 fusion.96
  104.0 0.6 multiply_reduce_fusion.26
  104.8 0.6 multiply_reduce_fusion.29
  105.6 0.2 and_select_fusion.10
  105.8 0.6 multiply_reduce_fusion.39
  106.5 0.2 fusion.53
  106.7 0.2 multiply_reduce_fusion.36
  107.0 1.9 %collective-permute-start.10 = (f32[7,16,1,128]{3,1,0,2:T(8,128)S(1)}, f32[7,16,1,128]{3,1,0,2:T(8,128)S(1)}, u32[]{:S(2)}, u32[]{:S(2)}) collective-permute-start(f32[7,16,1,128]{3,1,0,2:T(8,128)S(1)} %pad_maximum_fusion.4), channel_id=1, source_target_pairs={{0,1},{1,2},{2,3},{3,4},{4,5},{5,6},{6,7},{7,8},{8,9},{9,10},{10,1... | collective-permute-start | bytes 172040 | tf_op jit(solution)/shard_map/ppermute | solution.py:59
  108.9 8.0 %collective-permute-start.11 = (f32[7,16,1,128]{3,1,0,2:T(8,128)S(1)}, f32[7,16,1,128]{3,1,0,2:T(8,128)S(1)}, u32[]{:S(2)}, u32[]{:S(2)}) collective-permute-start(f32[7,16,1,128]{3,1,0,2:T(8,128)S(1)} %pad_maximum_fusion.4), channel_id=1, source_target_pairs={{1,0},{2,1},{3,2},{4,3},{5,4},{6,5},{7,6},{8,7},{9,8},{10,9},{11,1... | collective-permute-start | bytes 172040 | tf_op jit(solution)/shard_map/ppermute | solution.py:60
  117.6 1.0 collective-permute-done.11
  120.2 0.6 multiply_reduce_fusion.2
  120.8 0.2 and_select_fusion.21
  121.0 0.6 multiply_reduce_fusion.5
  121.6 0.2 and_select_fusion.3
  121.8 0.2 and_select_fusion.9
  122.0 0.7 multiply_reduce_fusion.15
  122.6 0.2 fusion.81
  122.8 0.2 multiply_reduce_fusion.12
  123.0 0.7 add_select_fusion
  123.8 30.7 %all-reduce = (f32[3,1,128]{2,1,0:T(1,128)S(1)}, f32[128]{0:T(128)S(1)}) all-reduce(f32[3,1,128]{2,1,0:T(1,128)S(1)} %reduce_sum.959, f32[128]{0:T(128)S(1)} %convert_bitcast_fusion), channel_id=1, replica_groups=mesh['group'=16,'brick'=32] {'group'}, use_global_device_ids=true, to_apply=%region_89.90 | all-reduce | flops 512 | bytes 4096 | tf_op jit(solution)/shard_map/psum | solution.py:212
  154.5 0.6 broadcast_multiply_fusion.2
  155.1 0.7 copy-done.19
  155.7 0.2 multiply_reduce_fusion.72
  155.9 0.3 fusion.220
  156.4 5.9 %collective-permute-start.12 = (f32[19,1,1,128]{3,2,1,0:T(1,128)S(1)}, f32[19,1,1,128]{3,2,1,0:T(1,128)S(1)}, u32[]{:S(2)}, u32[]{:S(2)}) collective-permute-start(f32[19,1,1,128]{3,2,1,0:T(1,128)S(1)} %get-tuple-element.207), channel_id=1, source_target_pairs={{0,32},{32,64},{64,96},{96,128},{128,160},{160,192},{192,224},{224... | collective-permute-start | bytes 29192 | tf_op jit(solution)/shard_map/ppermute | solution.py:59
  162.3 1.9 %collective-permute-start.13 = (f32[19,1,1,128]{3,2,1,0:T(1,128)S(1)}, f32[19,1,1,128]{3,2,1,0:T(1,128)S(1)}, u32[]{:S(2)}, u32[]{:S(2)}) collective-permute-start(f32[19,1,1,128]{3,2,1,0:T(1,128)S(1)} %get-tuple-element.208), channel_id=1, source_target_pairs={{32,0},{64,32},{96,64},{128,96},{160,128},{192,160},{224,192},{256... | collective-permute-start | bytes 29192 | tf_op jit(solution)/shard_map/ppermute | solution.py:60
  164.3 5.7 %collective-permute-done.13 = f32[19,1,1,128]{3,2,1,0:T(1,128)S(1)} collective-permute-done((f32[19,1,1,128]{3,2,1,0:T(1,128)S(1)}, f32[19,1,1,128]{3,2,1,0:T(1,128)S(1)}, u32[]{:S(2)}, u32[]{:S(2)}) %collective-permute-start.13) | collective-permute-done | bytes 9760 | tf_op jit(solution)/shard_map/ppermute | solution.py:60
  170.0 1.9 %collective-permute-start.14 = (f32[19,1,10,128]{3,2,1,0:T(8,128)S(1)}, f32[19,1,10,128]{3,2,1,0:T(8,128)S(1)}, u32[]{:S(2)}, u32[]{:S(2)}) collective-permute-start(f32[19,1,10,128]{3,2,1,0:T(8,128)S(1)} %pad_maximum_fusion.1), channel_id=1, source_target_pairs={{0,1},{1,2},{2,3},{3,4},{4,5},{5,6},{6,7},{7,8},{8,9},{9,10},{10,1... | collective-permute-start | bytes 291848 | tf_op jit(solution)/shard_map/ppermute | solution.py:59
  172.0 7.9 %collective-permute-start.15 = (f32[19,1,10,128]{3,2,1,0:T(8,128)S(1)}, f32[19,1,10,128]{3,2,1,0:T(8,128)S(1)}, u32[]{:S(2)}, u32[]{:S(2)}) collective-permute-start(f32[19,1,10,128]{3,2,1,0:T(8,128)S(1)} %pad_maximum_fusion.1), channel_id=1, source_target_pairs={{1,0},{2,1},{3,2},{4,3},{5,4},{6,5},{7,6},{8,7},{9,8},{10,9},{11,1... | collective-permute-start | bytes 291848 | tf_op jit(solution)/shard_map/ppermute | solution.py:60
  179.8 1.0 collective-permute-done.14
  180.8 1.8 collective-permute-done.15
  184.3 0.6 copy-done.17
  (259 shorter events, 12.5 us)
Async XLA Ops:
  0.6 0.8 copy-start
  0.6 0.8 copy-start.1
  1.4 24.3 %copy-start.2 = (f32[19,1,8,128]{3,2,1,0:T(8,128)S(1)}, f32[19,1,8,128]{3,2,1,0:T(8,128)}, u32[]{:S(2)}) copy-start(f32[19,1,8,128]{3,2,1,0:T(8,128)} %param.42) | copy-start | bytes 233476
  1.4 13.8 %copy-start.3 = (s32[1,16,1,128]{3,2,1,0:T(1,128)S(1)}, s32[1,16,1,128]{3,2,1,0:T(1,128)}, u32[]{:S(2)}) copy-start(s32[1,16,1,128]{3,2,1,0:T(1,128)} %param.47) | copy-start | bytes 24580
  1.4 82.1 %collective-permute-start.6 = (f32[7,16,1,128]{3,1,0,2:T(8,128)S(1)}, f32[7,16,1,128]{3,1,0,2:T(8,128)S(1)}, u32[]{:S(2)}, u32[]{:S(2)}) collective-permute-start(f32[7,16,1,128]{3,1,0,2:T(8,128)S(1)} %pad_maximum_fusion.2), channel_id=1, source_target_pairs={{1,0},{2,1},{3,2},{4,3},{5,4},{6,5},{7,6},{8,7},{9,8},{10,9},{11,1... | collective-permute-start | bytes 172040 | tf_op jit(solution)/shard_map/ppermute | solution.py:60
  13.3 70.3 %collective-permute-start.5 = (f32[7,16,1,128]{3,1,0,2:T(8,128)S(1)}, f32[7,16,1,128]{3,1,0,2:T(8,128)S(1)}, u32[]{:S(2)}, u32[]{:S(2)}) collective-permute-start(f32[7,16,1,128]{3,1,0,2:T(8,128)S(1)} %pad_maximum_fusion.2), channel_id=1, source_target_pairs={{0,1},{1,2},{2,3},{3,4},{4,5},{5,6},{6,7},{7,8},{8,9},{9,10},{10,1... | collective-permute-start | bytes 172040 | tf_op jit(solution)/shard_map/ppermute | solution.py:59
  15.2 0.7 copy-start.13
  15.8 49.9 %collective-permute-start.4 = (s32[16,1,128]{2,0,1:T(8,128)S(1)}, s32[16,1,128]{2,0,1:T(8,128)S(1)}, u32[]{:S(2)}, u32[]{:S(2)}) collective-permute-start(s32[16,1,128]{2,0,1:T(8,128)S(1)} %fusion.163), channel_id=1, source_target_pairs={{0,1},{1,2},{2,3},{3,4},{4,5},{5,6},{6,7},{7,8},{8,9},{9,10},{10,1... | collective-permute-start | bytes 24584 | tf_op jit(solution)/shard_map/ppermute | solution.py:59
  17.8 51.2 %collective-permute-start.7 = (s32[16,1,128]{2,0,1:T(8,128)S(1)}, s32[16,1,128]{2,0,1:T(8,128)S(1)}, u32[]{:S(2)}, u32[]{:S(2)}) collective-permute-start(s32[16,1,128]{2,0,1:T(8,128)S(1)} %fusion.163), channel_id=1, source_target_pairs={{1,0},{2,1},{3,2},{4,3},{5,4},{6,5},{7,6},{8,7},{9,8},{10,9},{11,1... | collective-permute-start | bytes 24584 | tf_op jit(solution)/shard_map/ppermute | solution.py:60
  25.6 0.7 copy-start.15
  26.5 0.7 copy-start.16
  27.1 0.7 copy-start.18
  27.2 0.7 copy-start.20
  28.1 0.7 copy-start.14
  29.1 40.2 %collective-permute-start = (f32[19,1,1,128]{3,2,1,0:T(1,128)S(1)}, f32[19,1,1,128]{3,2,1,0:T(1,128)S(1)}, u32[]{:S(2)}, u32[]{:S(2)}) collective-permute-start(f32[19,1,1,128]{3,2,1,0:T(1,128)S(1)} %get-tuple-element.211), channel_id=1, source_target_pairs={{0,32},{32,64},{64,96},{96,128},{128,160},{160,192},{192,224},{224... | collective-permute-start | bytes 29192 | tf_op jit(solution)/shard_map/ppermute | solution.py:59
  34.3 0.7 copy-start.4
  65.7 7.9 %collective-permute-start.1 = (f32[19,1,1,128]{3,2,1,0:T(1,128)S(1)}, f32[19,1,1,128]{3,2,1,0:T(1,128)S(1)}, u32[]{:S(2)}, u32[]{:S(2)}) collective-permute-start(f32[19,1,1,128]{3,2,1,0:T(1,128)S(1)} %get-tuple-element.212), channel_id=1, source_target_pairs={{32,0},{64,32},{96,64},{128,96},{160,128},{192,160},{224,192},{256... | collective-permute-start | bytes 29192 | tf_op jit(solution)/shard_map/ppermute | solution.py:60
  73.7 25.7 %collective-permute-start.2 = (f32[19,1,10,128]{3,2,1,0:T(8,128)S(1)}, f32[19,1,10,128]{3,2,1,0:T(8,128)S(1)}, u32[]{:S(2)}, u32[]{:S(2)}) collective-permute-start(f32[19,1,10,128]{3,2,1,0:T(8,128)S(1)} %pad_maximum_fusion), channel_id=1, source_target_pairs={{0,1},{1,2},{2,3},{3,4},{4,5},{5,6},{6,7},{7,8},{8,9},{9,10},{10,1... | collective-permute-start | bytes 291848 | tf_op jit(solution)/shard_map/ppermute | solution.py:59
  75.6 23.8 %collective-permute-start.3 = (f32[19,1,10,128]{3,2,1,0:T(8,128)S(1)}, f32[19,1,10,128]{3,2,1,0:T(8,128)S(1)}, u32[]{:S(2)}, u32[]{:S(2)}) collective-permute-start(f32[19,1,10,128]{3,2,1,0:T(8,128)S(1)} %pad_maximum_fusion), channel_id=1, source_target_pairs={{1,0},{2,1},{3,2},{4,3},{5,4},{6,5},{7,6},{8,7},{9,8},{10,9},{11,1... | collective-permute-start | bytes 291848 | tf_op jit(solution)/shard_map/ppermute | solution.py:60
  84.7 0.7 copy-start.11
  84.7 0.7 copy-start.12
  84.7 0.7 copy-start.8
  84.7 0.7 copy-start.9
  84.7 0.7 copy-start.10
  86.2 0.7 copy-start.5
  86.2 0.7 copy-start.6
  86.3 0.7 copy-start.7
  89.0 13.4 %collective-permute-start.8 = (f32[7,16,1,128]{3,1,0,2:T(8,128)S(1)}, f32[7,16,1,128]{3,1,0,2:T(8,128)S(1)}, u32[]{:S(2)}, u32[]{:S(2)}) collective-permute-start(f32[7,16,1,128]{3,1,0,2:T(8,128)S(1)} %pad_maximum_fusion.3), channel_id=1, source_target_pairs={{0,1},{1,2},{2,3},{3,4},{4,5},{5,6},{6,7},{7,8},{8,9},{9,10},{10,1... | collective-permute-start | bytes 172040 | tf_op jit(solution)/shard_map/ppermute | solution.py:59
  91.0 11.4 %collective-permute-start.9 = (f32[7,16,1,128]{3,1,0,2:T(8,128)S(1)}, f32[7,16,1,128]{3,1,0,2:T(8,128)S(1)}, u32[]{:S(2)}, u32[]{:S(2)}) collective-permute-start(f32[7,16,1,128]{3,1,0,2:T(8,128)S(1)} %pad_maximum_fusion.3), channel_id=1, source_target_pairs={{1,0},{2,1},{3,2},{4,3},{5,4},{6,5},{7,6},{8,7},{9,8},{10,9},{11,1... | collective-permute-start | bytes 172040 | tf_op jit(solution)/shard_map/ppermute | solution.py:60
  107.0 10.6 %collective-permute-start.10 = (f32[7,16,1,128]{3,1,0,2:T(8,128)S(1)}, f32[7,16,1,128]{3,1,0,2:T(8,128)S(1)}, u32[]{:S(2)}, u32[]{:S(2)}) collective-permute-start(f32[7,16,1,128]{3,1,0,2:T(8,128)S(1)} %pad_maximum_fusion.4), channel_id=1, source_target_pairs={{0,1},{1,2},{2,3},{3,4},{4,5},{5,6},{6,7},{7,8},{8,9},{9,10},{10,1... | collective-permute-start | bytes 172040 | tf_op jit(solution)/shard_map/ppermute | solution.py:59
  108.9 9.7 %collective-permute-start.11 = (f32[7,16,1,128]{3,1,0,2:T(8,128)S(1)}, f32[7,16,1,128]{3,1,0,2:T(8,128)S(1)}, u32[]{:S(2)}, u32[]{:S(2)}) collective-permute-start(f32[7,16,1,128]{3,1,0,2:T(8,128)S(1)} %pad_maximum_fusion.4), channel_id=1, source_target_pairs={{1,0},{2,1},{3,2},{4,3},{5,4},{6,5},{7,6},{8,7},{9,8},{10,9},{11,1... | collective-permute-start | bytes 172040 | tf_op jit(solution)/shard_map/ppermute | solution.py:60
  155.1 0.7 copy-start.19
  156.4 7.9 %collective-permute-start.12 = (f32[19,1,1,128]{3,2,1,0:T(1,128)S(1)}, f32[19,1,1,128]{3,2,1,0:T(1,128)S(1)}, u32[]{:S(2)}, u32[]{:S(2)}) collective-permute-start(f32[19,1,1,128]{3,2,1,0:T(1,128)S(1)} %get-tuple-element.207), channel_id=1, source_target_pairs={{0,32},{32,64},{64,96},{96,128},{128,160},{160,192},{192,224},{224... | collective-permute-start | bytes 29192 | tf_op jit(solution)/shard_map/ppermute | solution.py:59
  162.3 7.7 %collective-permute-start.13 = (f32[19,1,1,128]{3,2,1,0:T(1,128)S(1)}, f32[19,1,1,128]{3,2,1,0:T(1,128)S(1)}, u32[]{:S(2)}, u32[]{:S(2)}) collective-permute-start(f32[19,1,1,128]{3,2,1,0:T(1,128)S(1)} %get-tuple-element.208), channel_id=1, source_target_pairs={{32,0},{64,32},{96,64},{128,96},{160,128},{192,160},{224,192},{256... | collective-permute-start | bytes 29192 | tf_op jit(solution)/shard_map/ppermute | solution.py:60
  170.0 10.8 %collective-permute-start.14 = (f32[19,1,10,128]{3,2,1,0:T(8,128)S(1)}, f32[19,1,10,128]{3,2,1,0:T(8,128)S(1)}, u32[]{:S(2)}, u32[]{:S(2)}) collective-permute-start(f32[19,1,10,128]{3,2,1,0:T(8,128)S(1)} %pad_maximum_fusion.1), channel_id=1, source_target_pairs={{0,1},{1,2},{2,3},{3,4},{4,5},{5,6},{6,7},{7,8},{8,9},{9,10},{10,1... | collective-permute-start | bytes 291848 | tf_op jit(solution)/shard_map/ppermute | solution.py:59
  172.0 10.6 %collective-permute-start.15 = (f32[19,1,10,128]{3,2,1,0:T(8,128)S(1)}, f32[19,1,10,128]{3,2,1,0:T(8,128)S(1)}, u32[]{:S(2)}, u32[]{:S(2)}) collective-permute-start(f32[19,1,10,128]{3,2,1,0:T(8,128)S(1)} %pad_maximum_fusion.1), channel_id=1, source_target_pairs={{1,0},{2,1},{3,2},{4,3},{5,4},{6,5},{7,6},{8,7},{9,8},{10,9},{11,1... | collective-permute-start | bytes 291848 | tf_op jit(solution)/shard_map/ppermute | solution.py:60
  184.3 0.6 copy-start.17
where the time goes:
time: 186 us; the launch traced here: 185 us
  starting transfers between devices  78.3 us (42%)
  blocking collectives  61.1 us (33%)
  other arithmetic  17.4 us (9%)
  waiting for transfers between devices  13.7 us (7%)
  local copies, waits for them, and re-layouts  11.6 us (6%)
    ppermute x8, starting transfers between devices, extended(): after = lax.ppermute(leading, axis, down)  56.2 us
    psum x1, blocking collectives, local(): pooled_sum, pooled_count = lax.psum((speed_sum, count_value), 'group')  30.7 us
    psum x1, blocking collectives, local(): drag_velocity = lax.psum(owned, 'group')  30.4 us
    ppermute x8, starting transfers between devices, extended(): before = lax.ppermute(last, axis, up)  22.1 us
    ppermute x8, waiting for transfers between devices, extended(): after = lax.ppermute(leading, axis, down)  12.8 us
    unnamed x58, local copies, waits for them, and re-layouts  6.63 us
  transfers between devices with their start and end apart: 16, of which 5 were waited for; matrix products, arithmetic and copies ran while one was open for 6% of the time, Pallas kernels for 0%

commit v1 on v0

v1 whole, which is shorter than its diff:
```python
import math

import jax
import jax.numpy as jnp
import numpy as np
from jax import lax
from jax.experimental import pallas as pl
from jax.experimental.pallas import tpu as pltpu
from jax.sharding import PartitionSpec as P

VELOCITY_SET = (
    (0, 0, 0),
    (1, 0, 0),
    (-1, 0, 0),
    (0, 1, 0),
    (0, -1, 0),
    (0, 0, 1),
    (0, 0, -1),
    (1, 1, 0),
    (-1, -1, 0),
    (1, -1, 0),
    (-1, 1, 0),
    (1, 0, 1),
    (-1, 0, -1),
    (1, 0, -1),
    (-1, 0, 1),
    (0, 1, 1),
    (0, -1, -1),
    (0, 1, -1),
    (0, -1, 1),
)
WEIGHT_SET = (1.0 / 3.0,) + (1.0 / 18.0,) * 6 + (1.0 / 36.0,) * 12
OPPOSITE = (0, 2, 1, 4, 3, 6, 5, 8, 7, 10, 9, 12, 11, 14, 13, 16, 15, 18, 17)
Q = 19
TO_BRICK = ((1, 7, 9, 11, 13), (2, 8, 10, 12, 14))
TO_GROUP = ((3, 15, 17, 7, 10), (4, 16, 18, 9, 8))
RELAX_TIME = 0.8
PUSH = 0.001
VELOCITY_SCALE = 0.1
DRAG_RATE = 5.0
REPEL_SAME = 25.0
REPEL_CROSS = 50.0
FRICTION = 4.5
KICK_SCALE = 3.0 / math.sqrt(0.02) / math.sqrt(2.0)
TIME_STEP = 0.02
BOND_STIFF = 10.0
FAR = 1.0e8

GROUPS, BRICKS = 16, 32
CAP, NZ, LY, STEPS = 16, 128, 8, 3
MIDDLE = 7
MESH = pl.DeviceIdType.MESH
F32 = jnp.float32


def moments(g):
    def total(signs):
        parts = []
        for weight, members in ((1.0 / 18.0, range(1, 7)), (1.0 / 36.0, range(7, 19))):
            part = None
            for q in members:
                if signs[q]:
                    if part is None:
                        part = g[q] if signs[q] > 0 else -g[q]
                    else:
                        part = part + g[q] if signs[q] > 0 else part - g[q]
            parts.append(part * weight)
        return parts[0] + parts[1]

    density = g[0] * (1.0 / 3.0) + total((1,) * Q)
    inverse = 1.0 / density
    velocity = [total([c[axis] for c in VELOCITY_SET]) * inverse for axis in range(3)]
    return density, inverse, velocity


def along(q, s):
    value = None
    for axis in range(3):
        sign = VELOCITY_SET[q][axis]
        if sign:
            if value is None:
                value = s[axis] if sign > 0 else -s[axis]
            else:
                value = value + s[axis] if sign > 0 else value - s[axis]
    return value


def collide(g, density, inverse, velocity):
    s = [velocity[0] + (RELAX_TIME * PUSH) * inverse, velocity[1], velocity[2]]
    rest = 1.0 - 1.5 * (s[0] * s[0] + s[1] * s[1] + s[2] * s[2])
    post = []
    for q in range(Q):
        if q == 0:
            equilibrium = density * rest
        else:
            a = along(q, s)
            equilibrium = density * (rest + a * (3.0 + 4.5 * a))
        post.append(g[q] - (g[q] - equilibrium) * (1.0 / RELAX_TIME))
    return post


def kernel(
    pop_in,
    rows_in,
    pos_in,
    vel_in,
    kick_in,
    type_in,
    partner_in,
    count_in,
    pop_out,
    mean_out,
    pos_out,
    vel_out,
    cur,
    halo_kick,
    vel_send,
    halo_vel,
    near,
    drag,
    post,
    x_send,
    x_halo,
    row_send,
    row_halo,
    cells,
    sums,
    means,
    sem_cur,
    sem_kick,
    sem_vel,
    sem_drag,
    sem_x,
    sem_row,
    sem_cell,
    sem_sum,
    sem_mean,
):
    me_g = lax.axis_index("group")
    me_b = lax.axis_index("brick")
    up_b = lax.rem(me_b + 1, BRICKS)
    dn_b = lax.rem(me_b + BRICKS - 1, BRICKS)
    up_g = lax.rem(me_g + 1, GROUPS)
    dn_g = lax.rem(me_g + GROUPS - 1, GROUPS)
    is_mid = (me_g == MIDDLE) | (me_g == MIDDLE + 1)
    mid = jnp.where(me_g == MIDDLE, 0, 1)
    peers = [(lax.rem(me_g + k, GROUPS), me_b) for k in range(1, GROUPS)]
    beside = [(me_g, up_b), (me_g, dn_b)]
    corners = [(up_g, up_b), (up_g, dn_b), (dn_g, up_b), (dn_g, dn_b)]

    barrier = pltpu.get_barrier_semaphore()
    partners = peers + beside + corners
    for device in partners:
        pl.semaphore_signal(barrier, inc=1, device_id=device, device_id_type=MESH)

    unsent = []

    def remote(src, dst, send_sem, recv_sem, device):
        return pltpu.make_async_remote_copy(
            src_ref=src,
            dst_ref=dst,
            send_sem=send_sem,
            recv_sem=recv_sem,
            device_id=device,
            device_id_type=MESH,
        )

    def send(*args):
        copy = remote(*args)
        copy.start()
        unsent.append(copy)
        return copy

    row_ids = me_g * LY + lax.broadcasted_iota(jnp.int32, (LY, NZ), 0)
    at_cell = row_ids == rows_in[...]
    first_row = lax.broadcasted_iota(jnp.int32, (LY, NZ), 0) == 0
    last_row = lax.broadcasted_iota(jnp.int32, (LY, NZ), 0) == LY - 1
    low_wall = first_row & (me_g == 0)
    high_wall = last_row & (me_g == GROUPS - 1)

    slot_ids = lax.broadcasted_iota(jnp.int32, (CAP, NZ), 0)
    count = count_in[...]
    occupied = slot_ids < count
    tails = type_in[...].astype(F32)
    own_tail = type_in[...] == 1
    partner = partner_in[...]
    partner = jnp.where(partner < count, partner, slot_ids)
    cur[0, 0] = jnp.where(occupied, pos_in[0], FAR)
    cur[0, 1] = pos_in[1]
    cur[0, 2] = pos_in[2]
    for axis in range(3):
        cur[0, 3 + axis] = vel_in[axis]
    cur[0, 6] = kick_in[0]
    cur[0, 7] = tails

    g = [pop_in[q] for q in range(Q)]
    density, inverse, velocity = moments(g)

    @pl.when(is_mid)
    def _():
        for axis in range(3):
            drag[mid, axis : axis + 1, :] = jnp.sum(
                jnp.where(at_cell, velocity[axis], 0.0), axis=0, keepdims=True
            )

    def store_post(stage, values):
        for q in range(Q):
            post[stage, q] = values[q]
        for way in range(2):
            for n, q in enumerate(TO_BRICK[way]):
                x_send[stage, way, n] = values[q]
            edge = LY - 1 if way == 0 else 0
            for n, q in enumerate(TO_GROUP[way]):
                row_send[stage, way, n] = values[q][edge : edge + 1, :]

    store_post(0, collide(g, density, inverse, velocity))

    pl.semaphore_wait(barrier, len(partners))

    cur_copies = [
        send(cur.at[0], cur.at[2 - way], sem_cur.at[0, way], sem_cur.at[1, way], beside[way])
        for way in range(2)
    ]

    @pl.when(is_mid)
    def _():
        copies = [
            remote(drag.at[mid], drag.at[mid], sem_drag.at[k], sem_drag.at[16 + mid], peers[k])
            for k in range(GROUPS - 1)
        ]
        for copy in copies:
            copy.start()

    kick_copies = [
        send(
            kick_in.at[pl.ds(1, 2)],
            halo_kick.at[1 - way],
            sem_kick.at[0, way],
            sem_kick.at[1, way],
            beside[way],
        )
        for way in range(2)
    ]

    def send_post(stage):
        copies = []
        for way in range(2):
            copies.append(
                send(
                    x_send.at[stage, way],
                    x_halo.at[stage, way],
                    sem_x.at[0, stage, way],
                    sem_x.at[1, stage, way],
                    beside[way],
                )
            )
        for way in range(2):
            group = (up_g, dn_g)[way]
            for n, (start, size, brick) in enumerate(((0, 3, me_b), (3, 1, up_b), (4, 1, dn_b))):
                copies.append(
                    send(
                        row_send.at[stage, way, pl.ds(start, size)],
                        row_halo.at[stage, way, pl.ds(start, size)],
                        sem_row.at[0, stage, way, n],
                        sem_row.at[1, stage, way, n],
                        (group, brick),
                    )
                )
        return copies

    def stream(stage):
        moved = []
        for q in range(Q):
            cx, cy, cz = VELOCITY_SET[q]
            if cx == 0:
                value = post[stage, q]
            else:
                way = 0 if cx > 0 else 1
                value = x_halo[stage, way, TO_BRICK[way].index(q)]
            if cy:
                way = 0 if cy > 0 else 1
                edge = row_halo[stage, way, TO_GROUP[way].index(q)]
                value = pltpu.roll(value, 1 if cy > 0 else LY - 1, 0)
                value = jnp.where(first_row if cy > 0 else last_row, edge, value)
            if cz:
                value = pltpu.roll(value, 1 if cz > 0 else NZ - 1, 1)
            if cy:
                value = jnp.where(
                    low_wall if cy > 0 else high_wall, post[stage, OPPOSITE[q]], value
                )
            moved.append(value)
        return moved

    post_copies = send_post(0)

    def load_near(step, k):
        shift = (0.0, 1.0, -1.0)[k]
        places = [cur[k, axis] for axis in range(3)]
        if k == 0 or step == 0:
            speeds = [cur[k, 3 + axis] for axis in range(3)]
        else:
            speeds = [halo_vel[step - 1, k - 1, axis] for axis in range(3)]
            places = [p + TIME_STEP * v for p, v in zip(places, speeds)]
            if step < STEPS - 1:
                for axis in range(3):
                    cur[k, axis] = places[axis]
        if step == 0:
            kick = cur[k, 6]
        elif k == 0:
            kick = kick_in[step]
        else:
            kick = halo_kick[k - 1, step - 1]
        tail = cur[k, 7]
        push = KICK_SCALE * kick
        fields = [
            places[0] + shift,
            places[1],
            places[2],
            FRICTION * speeds[0],
            FRICTION * speeds[1],
            FRICTION * speeds[2],
            push + (REPEL_SAME + (REPEL_CROSS - REPEL_SAME) * tail),
            push + (REPEL_CROSS + (REPEL_SAME - REPEL_CROSS) * tail),
        ]
        for n, b in enumerate((-1, 0, 1)):
            for f, field in enumerate(fields):
                if b:
                    field = pltpu.roll(field, (-b) % NZ, 1)
                if f == 2:
                    field = field + float(b)
                near[n, f] = field

    def add_forces(step, totals):
        xi, yi, zi = [cur[0, axis] for axis in range(3)]
        ui, vi, wi = [FRICTION * cur[0, 3 + axis] for axis in range(3)]
        ki = KICK_SCALE * kick_in[step]

        def tile(n, totals):
            fx, fy, fz = totals
            for j in range(CAP):
                xj, yj, zj, uj, vj, wj, a0, a1 = [near[n, f, j : j + 1, :] for f in range(8)]
                dx = xi - xj
                dy = yi - yj
                dz = zi - zj
                weight = jnp.maximum(1.0 - (dx * dx + dy * dy + dz * dz), 0.0)
                closing = dx * (ui - uj) + dy * (vi - vj) + dz * (wi - wj)
                lift = jnp.where(own_tail, a1, a0) + ki
                strength = weight * (lift - weight * closing)
                fx = fx + strength * dx
                fy = fy + strength * dy
                fz = fz + strength * dz
            return fx, fy, fz

        return lax.fori_loop(0, 3, tile, totals)

    def bond_forces():
        places = [cur[0, axis] for axis in range(3)]
        found = list(places)
        for j in range(CAP):
            match = partner == j
            for axis in range(3):
                found[axis] = jnp.where(match, cur[0, axis, j : j + 1, :], found[axis])
        return tuple(-BOND_STIFF * (p - f) for p, f in zip(places, found))

    def cell_copies():
        other = MIDDLE + 1 - mid
        targets = [(other, me_b, 0), (me_g, up_b, 2), (other, up_b, 2)]
        targets += [(me_g, dn_b, 1), (other, dn_b, 1)]
        copies = []
        for n, (group, brick, column) in enumerate(targets):
            copies.append(
                remote(
                    cells.at[0, mid],
                    cells.at[column, mid],
                    sem_cell.at[n],
                    sem_cell.at[5 + 2 * column + mid],
                    (group, brick),
                )
            )
        return copies

    vel_copies = None
    for step in range(STEPS):
        totals = bond_forces()
        load_near(step, 0)
        totals = add_forces(step, totals)
        if step == 1:
            for copy in post_copies:
                copy.wait_recv()
            g = stream(0)
            density, inverse, velocity = moments(g)
            store_post(1, collide(g, density, inverse, velocity))
            post_copies = send_post(1)

            @pl.when(is_mid)
            def _():
                for n, value in enumerate([density] + velocity + [row_ids.astype(F32)]):
                    cells[0, mid, n : n + 1, :] = jnp.sum(
                        jnp.where(at_cell, value, 0.0), axis=0, keepdims=True
                    )
                for copy in cell_copies():
                    copy.start()

        if step == 2:
            for copy in post_copies:
                copy.wait_recv()
            g = stream(1)
            for q in range(Q):
                pop_out[q] = g[q]
        for k in (1, 2):
            if step == 0:
                cur_copies[2 - k].wait_recv()
            else:
                vel_copies[2 - k].wait_recv()
            if step == 1:
                kick_copies[2 - k].wait_recv()
            load_near(step, k)
            totals = add_forces(step, totals)
        if step == 0:
            for n in range(2):

                @pl.when(me_g != MIDDLE + n)
                def _():
                    remote(
                        drag.at[n], drag.at[n], sem_drag.at[0], sem_drag.at[16 + n], peers[0]
                    ).wait_recv()

            flow = (DRAG_RATE / VELOCITY_SCALE) * (drag[0, 0:3] + drag[1, 0:3])
            for copy in cur_copies:
                copy.wait_send()
        last = step == STEPS - 1
        for axis in range(3):
            speed = cur[0, 3 + axis]
            force = totals[axis] + (flow[axis : axis + 1] - DRAG_RATE * speed)
            speed = jnp.where(occupied, speed + TIME_STEP * force, 0.0)
            place = cur[0, axis] + TIME_STEP * speed
            if last:
                vel_out[axis] = speed
                pos_out[axis] = jnp.where(occupied, place, 0.0)
                sums[me_g, axis : axis + 1, :] = jnp.sum(speed, axis=0, keepdims=True)
            else:
                cur[0, 3 + axis] = speed
                cur[0, axis] = place
                vel_send[step, axis] = speed
        if last:
            sums[me_g, 3:4, :] = count.astype(F32)
        else:
            vel_copies = [
                send(
                    vel_send.at[step],
                    halo_vel.at[step, 1 - way],
                    sem_vel.at[0, step, way],
                    sem_vel.at[1, step, way],
                    beside[way],
                )
                for way in range(2)
            ]

    for k in range(GROUPS - 1):
        send(sums.at[me_g], sums.at[me_g], sem_sum.at[0, k], sem_sum.at[1, me_g], peers[k])
    for k in range(GROUPS - 1):
        other = peers[k][0]
        remote(
            sums.at[other], sums.at[other], sem_sum.at[0, k], sem_sum.at[1, other], peers[k]
        ).wait_recv()
    pooled = sums[0]
    for n in range(1, GROUPS):
        pooled = pooled + sums[n]
    mean = pooled[0:3] / pooled[3:4]
    mean_out[...] = mean

    @pl.when(is_mid)
    def _():
        means[2, 0:3] = mean
        mean_copies = [
            remote(means.at[2], means.at[1 - way], sem_mean.at[0, way], sem_mean.at[1, way], beside[way])
            for way in range(2)
        ]
        for copy in mean_copies:
            copy.start()
        for column in range(3):
            for n in range(2):
                wait = remote(
                    cells.at[0, mid],
                    cells.at[column, n],
                    sem_cell.at[0],
                    sem_cell.at[5 + 2 * column + n],
                    beside[0],
                )
                if column:
                    wait.wait_recv()
                else:

                    @pl.when(mid != n)
                    def _():
                        wait.wait_recv()

        def change(column, column_mean, members):
            cell = cells[column, 0] + cells[column, 1]
            density = cell[0:1]
            inverse = 1.0 / density
            row = cell[4:5].astype(jnp.int32)
            before, after = [], []
            for axis in range(3):
                speed = cell[1 + axis : 2 + axis]
                force = VELOCITY_SCALE * column_mean[axis : axis + 1] - speed
                pushed = speed + (RELAX_TIME * PUSH) * inverse if axis == 0 else speed
                before.append(pushed)
                after.append(pushed + RELAX_TIME * force * inverse)
            square = sum(a * a - b * b for a, b in zip(after, before))
            for q in members:
                cx, cy, cz = VELOCITY_SET[q]
                change = -1.5 * square
                if q:
                    a, b = along(q, after), along(q, before)
                    change = change + (a - b) * (3.0 + 4.5 * (a + b))
                change = (1.0 / RELAX_TIME) * density * change
                tile = jnp.where(row_ids == row + cy, change, 0.0)
                if cz:
                    tile = pltpu.roll(tile, 1 if cz > 0 else NZ - 1, 1)
                pop_out[q] += tile

        change(0, mean, [q for q in range(Q) if VELOCITY_SET[q][0] == 0])
        for way in range(2):
            mean_copies[way].wait_recv()
            change(2 - way, means[1 - way], TO_BRICK[way])
        for copy in mean_copies:
            copy.wait_send()
        for copy in cell_copies():
            copy.wait_send()
        for k in range(GROUPS - 1):
            remote(
                drag.at[mid], drag.at[mid], sem_drag.at[k], sem_drag.at[16 + mid], peers[k]
            ).wait_send()

    for copy in unsent:
        if not any(copy is other for other in cur_copies):
            copy.wait_send()


def local(
    populations, membrane_rows, positions, velocities, kicks, bead_types, bond_partner, tile_counts
):
    vmem = pl.BlockSpec(memory_space=pltpu.VMEM)
    dma = pltpu.SemaphoreType.DMA
    bead = (CAP, NZ)
    outs = pl.pallas_call(
        kernel,
        out_shape=(
            jax.ShapeDtypeStruct((Q, LY, NZ), F32),
            jax.ShapeDtypeStruct((3, NZ), F32),
            jax.ShapeDtypeStruct((3, *bead), F32),
            jax.ShapeDtypeStruct((3, *bead), F32),
        ),
        in_specs=[vmem] * 8,
        out_specs=[vmem] * 4,
        scratch_shapes=[
            pltpu.VMEM((3, 8, *bead), F32),
            pltpu.VMEM((2, 2, *bead), F32),
            pltpu.VMEM((2, 3, *bead), F32),
            pltpu.VMEM((2, 2, 3, *bead), F32),
            pltpu.VMEM((3, 8, *bead), F32),
            pltpu.VMEM((2, 8, NZ), F32),
            pltpu.VMEM((2, Q, LY, NZ), F32),
            pltpu.VMEM((2, 2, 5, LY, NZ), F32),
            pltpu.VMEM((2, 2, 5, LY, NZ), F32),
            pltpu.VMEM((2, 2, 5, 1, NZ), F32),
            pltpu.VMEM((2, 2, 5, 1, NZ), F32),
            pltpu.VMEM((3, 2, 8, NZ), F32),
            pltpu.VMEM((GROUPS, 4, NZ), F32),
            pltpu.VMEM((3, 8, NZ), F32),
            dma((2, 2)),
            dma((2, 2)),
            dma((2, 2, 2)),
            dma((18,)),
            dma((2, 2, 2)),
            dma((2, 2, 2, 3)),
            dma((11,)),
            dma((2, GROUPS)),
            dma((2, 2)),
        ],
        compiler_params=pltpu.CompilerParams(collective_id=0, has_side_effects=True),
        name="cycle",
    )(
        populations.reshape(Q, LY, NZ),
        membrane_rows,
        positions.reshape(3, *bead),
        velocities.reshape(3, *bead),
        kicks.reshape(STEPS, *bead),
        bead_types.reshape(bead),
        bond_partner.reshape(bead),
        tile_counts.reshape(1, NZ),
    )
    second, mean, places, speeds = outs
    return (
        second.reshape(Q, 1, LY, NZ),
        mean.reshape(3, 1, NZ),
        places.reshape(1, 3, CAP, 1, NZ),
        speeds.reshape(1, 3, CAP, 1, NZ),
    )


def solution(mesh):
    return jax.shard_map(
        local,
        mesh=mesh,
        in_specs=(
            P(None, "brick", "group", None),
            P("brick", None),
            P("group", None, None, "brick", None),
            P("group", None, None, "brick", None),
            P("group", None, None, "brick", None),
            P("group", None, "brick", None),
            P("group", None, "brick", None),
            P("group", "brick", None),
        ),
        out_specs=(
            P(None, "brick", "group", None),
            P(None, "brick", None),
            P("group", None, None, "brick", None),
            P("group", None, None, "brick", None),
        ),
        check_vma=False,
    )
```

time: 186 us -> 45.2 us (0.24)
  starting transfers between devices: 78.3 us -> 0 us
  blocking collectives: 61.1 us -> 0 us
  Pallas kernels: 0 us -> 40.2 us
  other arithmetic: 17.4 us -> 0 us
  waiting for transfers between devices: 13.7 us -> 0 us
  local copies, waits for them, and re-layouts: 11.6 us -> 4.1 us
    ppermute x16 -> x0, starting transfers between devices: 78.3 us -> none  [the longest x8 56.2 us: extended(): after = lax.ppermute(leading, axis, down)]
    psum x2 -> x0, blocking collectives: 61.1 us -> none  [the longest x1 30.7 us: local(): pooled_sum, pooled_count = lax.psum((speed_sum, count_value), 'group')]
    pallas_call x0 -> x1, Pallas kernels: none -> 40.2 us  [local(): pl.pallas_call(kernel, out_shape=(jax.ShapeDtypeStruct((Q, LY, NZ), F32),...]
    ppermute x16 -> x0, waiting for transfers between devices: 13.7 us -> none  [the longest x8 12.8 us: extended(): after = lax.ppermute(leading, axis, down)]
    reduce_sum x13 -> x0, other arithmetic: 6.32 us -> none  [the longest x6 3.71 us: bead_forces(): dist_sq = jnp.sum(apart * apart, axis=0)]
    slice x50 -> x0, local copies, waits for them, and re-layouts: 3.61 us -> none  [the longest x36 2.73 us: slab_pick(): jnp.roll(array[..., 1 + shift_x:1 + shift_x + width, :], -shift_z, axis=-1)]
    select_n x14 -> x0, other arithmetic: 2.87 us -> none  [the longest x12 2.18 us: bead_forces(): jnp.where(paired, repel * weight - FRICTION * weight * weight * closing +...]
    unnamed x35 -> x0, other arithmetic: 2.58 us -> none
  transfers between devices with their start and end apart: 16 -> 0, of which waited for: 5 -> 0; matrix products, arithmetic and copies ran while one was open for 6% -> 0% of each run, Pallas kernels for 0% -> 0%
where the time goes in v1:
time: 45.2 us; the launch traced here: 44.9 us
  Pallas kernels  40.2 us (89%)
  local copies, waits for them, and re-layouts  4.1 us (9%)
  between operations  0.65 us (1%)
    pallas_call x1, Pallas kernels, local(): pl.pallas_call(kernel, out_shape=(jax.ShapeDtypeStruct((Q, LY, NZ), F32),...  40.2 us
    unnamed x10, local copies, waits for them, and re-layouts  4.1 us

profile of v1, /device:TPU:88, one launch (start us, length us, event | category | flops | bytes accessed | tf_op | source)
XLA Modules:
  0.0 44.9 jit_solution(3251724321289141608)
XLA Ops:
  0.6 40.2 %cycle.1 = (f32[19,8,128]{2,1,0:T(8,128)}, f32[3,128]{1,0:T(4,128)}, f32[3,16,128]{2,1,0:T(8,128)}, f32[3,16,128]{2,1,0:T(8,128)}) custom-call(f32[19,8,128]{2,1,0:T(8,128)} %bitcast.17, s32[1,128]{1,0:T(1,128)} %rows_in.1, f32[3,16,128]{2,1,0:T(8,128)} %bitcast.21, f32[3,16,128]{2,1,0:T(8,128)} %bitcast.22, f32[3,16,128]{2,1,0:T(8,128)} %bitcast.23, ...), custom_call_target="tpu_custom_call" | custom-call | tf_op jit(solution)/shard_map/cycle/pallas_call | solution.py:547
  40.8 0.0 copy-start.2
  40.8 0.6 %copy-done.2 = f32[3,128]{1,0:T(4,128)S(1)} copy-done((f32[3,128]{1,0:T(4,128)S(1)}, f32[3,128]{1,0:T(4,128)}, u32[]{:S(2)}) %copy-start.2) | copy-done | bytes 1560
  41.5 0.6 %copy.13 = f32[3,1,128]{2,1,0:T(1,128)} copy(f32[3,1,128]{2,0,1:T(4,128)S(1)} %bitcast.26) | data formatting | bytes 3072
  42.1 0.0 copy-start.1
  42.1 1.5 %copy.19 = f32[19,1,8,128]{3,2,1,0:T(8,128)} copy(f32[19,1,8,128]{3,2,1,0:T(8,128)} %bitcast.18) | data formatting | bytes 155648
  43.6 0.0 copy-done.1
  43.6 0.0 copy-start
  43.6 0.6 %copy.20 = f32[1,3,16,1,128]{4,3,2,1,0:T(1,128)} copy(f32[1,3,16,1,128]{4,3,2,1,0:T(1,128)S(1)} %bitcast.20) | data formatting | bytes 49152
  44.2 0.1 copy-done
  44.3 0.6 %copy.21 = f32[1,3,16,1,128]{4,3,2,1,0:T(1,128)} copy(f32[1,3,16,1,128]{4,3,2,1,0:T(1,128)S(1)} %bitcast.19) | data formatting | bytes 49152
Async XLA Ops:
  40.8 0.7 %copy-start.2 = (f32[3,128]{1,0:T(4,128)S(1)}, f32[3,128]{1,0:T(4,128)}, u32[]{:S(2)}) copy-start(f32[3,128]{1,0:T(4,128)} %get-tuple-element.9) | copy-start | bytes 4612
  42.1 1.5 %copy-start.1 = (f32[3,16,128]{2,1,0:T(8,128)S(1)}, f32[3,16,128]{2,1,0:T(8,128)}, u32[]{:S(2)}) copy-start(f32[3,16,128]{2,1,0:T(8,128)} %get-tuple-element.10) | copy-start | bytes 73732
  43.6 0.7 %copy-start = (f32[3,16,128]{2,1,0:T(8,128)S(1)}, f32[3,16,128]{2,1,0:T(8,128)}, u32[]{:S(2)}) copy-start(f32[3,16,128]{2,1,0:T(8,128)} %get-tuple-element.11) | copy-start | bytes 73732

commit v2 on v1

--- a/solution.py
+++ b/solution.py
@@ -100,6 +100,18 @@
 
 
 def kernel(
+    pop_hbm,
+    rows_hbm,
+    pos_hbm,
+    vel_hbm,
+    kick_hbm,
+    type_hbm,
+    partner_hbm,
+    count_hbm,
+    pop_out,
+    mean_out,
+    pos_out,
+    vel_out,
     pop_in,
     rows_in,
     pos_in,
@@ -108,10 +120,7 @@
     type_in,
     partner_in,
     count_in,
-    pop_out,
-    mean_out,
-    pos_out,
-    vel_out,
+    sem_in,
     cur,
     halo_kick,
     vel_send,
@@ -146,12 +155,31 @@
     mid = jnp.where(me_g == MIDDLE, 0, 1)
     peers = [(lax.rem(me_g + k, GROUPS), me_b) for k in range(1, GROUPS)]
     beside = [(me_g, up_b), (me_g, dn_b)]
+    even = lax.rem(me_b, 2) == 0
+    pair = [(me_g, jnp.where(even, up_b, dn_b)), (me_g, jnp.where(even, dn_b, up_b))]
+    side = jnp.where(even, 1.0, -1.0)
     corners = [(up_g, up_b), (up_g, dn_b), (dn_g, up_b), (dn_g, dn_b)]
 
     barrier = pltpu.get_barrier_semaphore()
     partners = peers + beside + corners
     for device in partners:
         pl.semaphore_signal(barrier, inc=1, device_id=device, device_id_type=MESH)
+
+    loads = {}
+    for n, (name, source, target) in enumerate(
+        (
+            ("pos", pos_hbm, pos_in),
+            ("vel", vel_hbm, vel_in),
+            ("kick", kick_hbm, kick_in),
+            ("type", type_hbm, type_in),
+            ("count", count_hbm, count_in),
+            ("partner", partner_hbm, partner_in),
+            ("pop", pop_hbm, pop_in),
+            ("rows", rows_hbm, rows_in),
+        )
+    ):
+        loads[name] = pltpu.make_async_copy(source, target, sem_in.at[n])
+        loads[name].start()
 
     unsent = []
 
@@ -171,13 +199,8 @@
         unsent.append(copy)
         return copy
 
-    row_ids = me_g * LY + lax.broadcasted_iota(jnp.int32, (LY, NZ), 0)
-    at_cell = row_ids == rows_in[...]
-    first_row = lax.broadcasted_iota(jnp.int32, (LY, NZ), 0) == 0
-    last_row = lax.broadcasted_iota(jnp.int32, (LY, NZ), 0) == LY - 1
-    low_wall = first_row & (me_g == 0)
-    high_wall = last_row & (me_g == GROUPS - 1)
-
+    for name in ("pos", "vel", "kick", "type", "count", "partner"):
+        loads[name].wait()
     slot_ids = lax.broadcasted_iota(jnp.int32, (CAP, NZ), 0)
     count = count_in[...]
     occupied = slot_ids < count
@@ -193,6 +216,22 @@
     cur[0, 6] = kick_in[0]
     cur[0, 7] = tails
 
+    pl.semaphore_wait(barrier, len(partners))
+
+    cur_copies = [
+        send(cur.at[0], cur.at[1 + way], sem_cur.at[0, way], sem_cur.at[1, way], pair[way])
+        for way in range(2)
+    ]
+
+    row_ids = me_g * LY + lax.broadcasted_iota(jnp.int32, (LY, NZ), 0)
+    first_row = lax.broadcasted_iota(jnp.int32, (LY, NZ), 0) == 0
+    last_row = lax.broadcasted_iota(jnp.int32, (LY, NZ), 0) == LY - 1
+    low_wall = first_row & (me_g == 0)
+    high_wall = last_row & (me_g == GROUPS - 1)
+
+    for name in ("pop", "rows"):
+        loads[name].wait()
+    at_cell = row_ids == rows_in[...]
     g = [pop_in[q] for q in range(Q)]
     density, inverse, velocity = moments(g)
 
@@ -215,13 +254,6 @@
 
     store_post(0, collide(g, density, inverse, velocity))
 
-    pl.semaphore_wait(barrier, len(partners))
-
-    cur_copies = [
-        send(cur.at[0], cur.at[2 - way], sem_cur.at[0, way], sem_cur.at[1, way], beside[way])
-        for way in range(2)
-    ]
-
     @pl.when(is_mid)
     def _():
         copies = [
@@ -234,10 +266,10 @@
     kick_copies = [
         send(
             kick_in.at[pl.ds(1, 2)],
-            halo_kick.at[1 - way],
+            halo_kick.at[way],
             sem_kick.at[0, way],
             sem_kick.at[1, way],
-            beside[way],
+            pair[way],
         )
         for way in range(2)
     ]
@@ -294,7 +326,7 @@
     post_copies = send_post(0)
 
     def load_near(step, k):
-        shift = (0.0, 1.0, -1.0)[k]
+        shift = (0.0, side, -side)[k]
         places = [cur[k, axis] for axis in range(3)]
         if k == 0 or step == 0:
             speeds = [cur[k, 3 + axis] for axis in range(3)]
@@ -409,11 +441,11 @@
                 pop_out[q] = g[q]
         for k in (1, 2):
             if step == 0:
-                cur_copies[2 - k].wait_recv()
+                cur_copies[k - 1].wait_recv()
             else:
-                vel_copies[2 - k].wait_recv()
+                vel_copies[k - 1].wait_recv()
             if step == 1:
-                kick_copies[2 - k].wait_recv()
+                kick_copies[k - 1].wait_recv()
             load_near(step, k)
             totals = add_forces(step, totals)
         if step == 0:
@@ -448,10 +480,10 @@
             vel_copies = [
                 send(
                     vel_send.at[step],
-                    halo_vel.at[step, 1 - way],
+                    halo_vel.at[step, way],
                     sem_vel.at[0, step, way],
                     sem_vel.at[1, step, way],
-                    beside[way],
+                    pair[way],
                 )
                 for way in range(2)
             ]
@@ -467,7 +499,8 @@
     for n in range(1, GROUPS):
         pooled = pooled + sums[n]
     mean = pooled[0:3] / pooled[3:4]
-    mean_out[...] = mean
+    for axis in range(3):
+        mean_out[axis] = mean[axis : axis + 1]
 
     @pl.when(is_mid)
     def _():
@@ -538,23 +571,46 @@
             copy.wait_send()
 
 
+def hand_out(*refs):
+    sources, targets, sem = refs[:4], refs[4:8], refs[8]
+    copies = [
+        pltpu.make_async_copy(source, target, sem.at[n])
+        for n, (source, target) in enumerate(zip(sources, targets))
+    ]
+    for copy in copies:
+        copy.start()
+    for copy in copies:
+        copy.wait()
+
+
 def local(
     populations, membrane_rows, positions, velocities, kicks, bead_types, bond_partner, tile_counts
 ):
     vmem = pl.BlockSpec(memory_space=pltpu.VMEM)
+    hbm = pl.BlockSpec(memory_space=pltpu.HBM)
+    anywhere = pl.BlockSpec(memory_space=pl.ANY)
     dma = pltpu.SemaphoreType.DMA
     bead = (CAP, NZ)
     outs = pl.pallas_call(
         kernel,
         out_shape=(
-            jax.ShapeDtypeStruct((Q, LY, NZ), F32),
-            jax.ShapeDtypeStruct((3, NZ), F32),
-            jax.ShapeDtypeStruct((3, *bead), F32),
-            jax.ShapeDtypeStruct((3, *bead), F32),
+            pltpu.VMEM((Q, LY, NZ), F32),
+            pltpu.VMEM((3, 1, NZ), F32),
+            pltpu.VMEM((3, *bead), F32),
+            pltpu.VMEM((3, *bead), F32),
         ),
-        in_specs=[vmem] * 8,
+        in_specs=[hbm] * 8,
         out_specs=[vmem] * 4,
         scratch_shapes=[
+            pltpu.VMEM((Q, LY, NZ), F32),
+            pltpu.VMEM((1, NZ), jnp.int32),
+            pltpu.VMEM((3, *bead), F32),
+            pltpu.VMEM((3, *bead), F32),
+            pltpu.VMEM((STEPS, *bead), F32),
+            pltpu.VMEM(bead, jnp.int32),
+            pltpu.VMEM(bead, jnp.int32),
+            pltpu.VMEM((1, NZ), jnp.int32),
+            dma((8,)),
             pltpu.VMEM((3, 8, *bead), F32),
             pltpu.VMEM((2, 2, *bead), F32),
             pltpu.VMEM((2, 3, *bead), F32),
@@ -579,22 +635,37 @@
             dma((2, GROUPS)),
             dma((2, 2)),
         ],
-        compiler_params=pltpu.CompilerParams(collective_id=0, has_side_effects=True),
+        compiler_params=pltpu.CompilerParams(
+            collective_id=0, has_side_effects=True, vmem_limit_bytes=4 << 20
+        ),
         name="cycle",
     )(
-        populations.reshape(Q, LY, NZ),
-        membrane_rows,
-        positions.reshape(3, *bead),
-        velocities.reshape(3, *bead),
-        kicks.reshape(STEPS, *bead),
-        bead_types.reshape(bead),
-        bond_partner.reshape(bead),
-        tile_counts.reshape(1, NZ),
+        *(
+            pltpu.with_memory_space_constraint(x, pltpu.HBM)
+            for x in (
+                populations.reshape(Q, LY, NZ),
+                membrane_rows,
+                positions.reshape(3, *bead),
+                velocities.reshape(3, *bead),
+                kicks.reshape(STEPS, *bead),
+                bead_types.reshape(bead),
+                bond_partner.reshape(bead),
+                tile_counts.reshape(1, NZ),
+            )
+        )
     )
-    second, mean, places, speeds = outs
+    second, mean, places, speeds = pl.pallas_call(
+        hand_out,
+        out_shape=tuple(jax.ShapeDtypeStruct(x.shape, F32) for x in outs),
+        in_specs=[anywhere] * 4,
+        out_specs=[hbm] * 4,
+        scratch_shapes=[dma((4,))],
+        compiler_params=pltpu.CompilerParams(vmem_limit_bytes=1 << 20),
+        name="hand_out",
+    )(*outs)
     return (
         second.reshape(Q, 1, LY, NZ),
-        mean.reshape(3, 1, NZ),
+        mean,
         places.reshape(1, 3, CAP, 1, NZ),
         speeds.reshape(1, 3, CAP, 1, NZ),
     )

time: 45.2 us -> 39.3 us (0.87)
  local copies, waits for them, and re-layouts: 4.1 us -> 0 us
  Pallas kernels: 40.2 us -> 38.5 us
    unnamed x10 -> x0, local copies, waits for them, and re-layouts: 4.1 us -> none
    pallas_call x1 -> x2, Pallas kernels: 40.2 us -> 38.5 us  [the longest x1 37.9 us: local(): pl.pallas_call(kernel, out_shape=(pltpu.VMEM((Q, LY, NZ), F32), pltpu.VME...]
where the time goes in v2:
time: 39.3 us; the launch traced here: 39.2 us
  Pallas kernels  38.5 us (98%)
  between operations  0.64 us (2%)
    pallas_call x1, Pallas kernels, local(): pl.pallas_call(kernel, out_shape=(pltpu.VMEM((Q, LY, NZ), F32), pltpu.VME...  37.9 us

profile of v2, /device:TPU:88, one launch (start us, length us, event | category | flops | bytes accessed | tf_op | source)
XLA Modules:
  0.0 39.2 jit_solution(207687659038469289)
XLA Ops:
  0.6 37.9 %cycle.1 = (f32[19,8,128]{2,1,0:T(8,128)S(1)}, f32[3,1,128]{2,1,0:T(1,128)S(1)}, f32[3,16,128]{2,1,0:T(8,128)S(1)}, f32[3,16,128]{2,1,0:T(8,128)S(1)}) custom-call(f32[19,8,128]{2,1,0:T(8,128)} %bitcast.16, s32[1,128]{1,0:T(1,128)} %rows_hbm.1, f32[3,16,128]{2,1,0:T(8,128)} %bitcast.17, f32[3,16,128]{2,1,0:T(8,128)} %bitcast.18, f32[3,16,128]{2,1,0:T(8,128)} %bitcast.19, ...), custom_call_target="tpu_custom_call" | custom-call | tf_op jit(solution)/shard_map/cycle/pallas_call | solution.py:594
  38.5 0.7 %hand_out.1 = (f32[19,8,128]{2,1,0:T(8,128)}, f32[3,1,128]{2,1,0:T(1,128)}, f32[3,16,128]{2,1,0:T(8,128)}, f32[3,16,128]{2,1,0:T(8,128)}) custom-call(f32[19,8,128]{2,1,0:T(8,128)S(1)} %get-tuple-element.12.refs_0_, f32[3,1,128]{2,1,0:T(1,128)S(1)} %get-tuple-element.13.refs_1_, f32[3,16,128]{2,1,0:T(8,128)S(1)} %get-tuple-element.14.refs_2_, ...), custom_call_target="tpu_custom_call" | custom-call | tf_op jit(solution)/shard_map/hand_out/pallas_call | solution.py:657

commit v3 on v2

--- a/solution.py
+++ b/solution.py
@@ -49,6 +49,7 @@
 GROUPS, BRICKS = 16, 32
 CAP, NZ, LY, STEPS = 16, 128, 8, 3
 MIDDLE = 7
+FARTHEST = (8, 7, 9, 6, 10, 5, 11, 4, 12, 3, 13, 2, 14, 1, 15)
 MESH = pl.DeviceIdType.MESH
 F32 = jnp.float32
 
@@ -144,6 +145,8 @@
     sem_cell,
     sem_sum,
     sem_mean,
+    sem_entered,
+    sem_ready,
 ):
     me_g = lax.axis_index("group")
     me_b = lax.axis_index("brick")
@@ -160,10 +163,7 @@
     side = jnp.where(even, 1.0, -1.0)
     corners = [(up_g, up_b), (up_g, dn_b), (dn_g, up_b), (dn_g, dn_b)]
 
-    barrier = pltpu.get_barrier_semaphore()
-    partners = peers + beside + corners
-    for device in partners:
-        pl.semaphore_signal(barrier, inc=1, device_id=device, device_id_type=MESH)
+    far_mids = [(MIDDLE, pair[1][1]), (MIDDLE + 1, pair[1][1])]
 
     loads = {}
     for n, (name, source, target) in enumerate(
@@ -173,13 +173,18 @@
             ("kick", kick_hbm, kick_in),
             ("type", type_hbm, type_in),
             ("count", count_hbm, count_in),
-            ("partner", partner_hbm, partner_in),
             ("pop", pop_hbm, pop_in),
             ("rows", rows_hbm, rows_in),
+            ("partner", partner_hbm, partner_in),
         )
     ):
         loads[name] = pltpu.make_async_copy(source, target, sem_in.at[n])
         loads[name].start()
+
+    barrier = pltpu.get_barrier_semaphore()
+    partners = pair[::-1] + [peers[k - 1] for k in FARTHEST] + corners
+    for device in partners:
+        pl.semaphore_signal(barrier, inc=1, device_id=device, device_id_type=MESH)
 
     unsent = []
 
@@ -199,15 +204,13 @@
         unsent.append(copy)
         return copy
 
-    for name in ("pos", "vel", "kick", "type", "count", "partner"):
+    for name in ("pos", "vel", "kick", "type", "count"):
         loads[name].wait()
     slot_ids = lax.broadcasted_iota(jnp.int32, (CAP, NZ), 0)
     count = count_in[...]
     occupied = slot_ids < count
     tails = type_in[...].astype(F32)
     own_tail = type_in[...] == 1
-    partner = partner_in[...]
-    partner = jnp.where(partner < count, partner, slot_ids)
     cur[0, 0] = jnp.where(occupied, pos_in[0], FAR)
     cur[0, 1] = pos_in[1]
     cur[0, 2] = pos_in[2]
@@ -218,10 +221,18 @@
 
     pl.semaphore_wait(barrier, len(partners))
 
-    cur_copies = [
-        send(cur.at[0], cur.at[1 + way], sem_cur.at[0, way], sem_cur.at[1, way], pair[way])
-        for way in range(2)
-    ]
+    @pl.when(is_mid)
+    def _():
+        pl.semaphore_signal(sem_entered, inc=1, device_id=pair[1], device_id_type=MESH)
+
+    def send_pair(source, target, sems):
+        copies = [
+            send(source, target.at[way], sems.at[0, way], sems.at[1, way], pair[way])
+            for way in (1, 0)
+        ]
+        return copies[::-1]
+
+    cur_copies = send_pair(cur.at[0], cur.at[pl.ds(1, 2)], sem_cur)
 
     row_ids = me_g * LY + lax.broadcasted_iota(jnp.int32, (LY, NZ), 0)
     first_row = lax.broadcasted_iota(jnp.int32, (LY, NZ), 0) == 0
@@ -234,6 +245,12 @@
     at_cell = row_ids == rows_in[...]
     g = [pop_in[q] for q in range(Q)]
     density, inverse, velocity = moments(g)
+
+    def drag_copies():
+        return [
+            remote(drag.at[mid], drag.at[mid], sem_drag.at[k - 1], sem_drag.at[16 + mid], peers[k - 1])
+            for k in FARTHEST
+        ]
 
     @pl.when(is_mid)
     def _():
@@ -241,6 +258,10 @@
             drag[mid, axis : axis + 1, :] = jnp.sum(
                 jnp.where(at_cell, velocity[axis], 0.0), axis=0, keepdims=True
             )
+        for copy in drag_copies():
+            copy.start()
+
+    kick_copies = send_pair(kick_in.at[pl.ds(1, 2)], halo_kick, sem_kick)
 
     def store_post(stage, values):
         for q in range(Q):
@@ -253,26 +274,6 @@
                 row_send[stage, way, n] = values[q][edge : edge + 1, :]
 
     store_post(0, collide(g, density, inverse, velocity))
-
-    @pl.when(is_mid)
-    def _():
-        copies = [
-            remote(drag.at[mid], drag.at[mid], sem_drag.at[k], sem_drag.at[16 + mid], peers[k])
-            for k in range(GROUPS - 1)
-        ]
-        for copy in copies:
-            copy.start()
-
-    kick_copies = [
-        send(
-            kick_in.at[pl.ds(1, 2)],
-            halo_kick.at[way],
-            sem_kick.at[0, way],
-            sem_kick.at[1, way],
-            pair[way],
-        )
-        for way in range(2)
-    ]
 
     def send_post(stage):
         copies = []
@@ -383,7 +384,13 @@
                 fz = fz + strength * dz
             return fx, fy, fz
 
-        return lax.fori_loop(0, 3, tile, totals)
+        for n in range(3):
+            totals = tile(n, totals)
+        return totals
+
+    loads["partner"].wait()
+    partner = partner_in[...]
+    partner = jnp.where(partner < count, partner, slot_ids)
 
     def bond_forces():
         places = [cur[0, axis] for axis in range(3)]
@@ -411,39 +418,39 @@
             )
         return copies
 
-    vel_copies = None
+    def lattice_between():
+        for copy in post_copies:
+            copy.wait_recv()
+        g = stream(0)
+        density, inverse, velocity = moments(g)
+        store_post(1, collide(g, density, inverse, velocity))
+        copies = send_post(1)
+
+        @pl.when(is_mid)
+        def _():
+            pl.semaphore_wait(sem_entered, 1)
+            for n in range(GROUPS):
+                pl.semaphore_signal(
+                    sem_ready, inc=1, device_id=(n, pair[1][1]), device_id_type=MESH
+                )
+            for n, value in enumerate([density] + velocity + [row_ids.astype(F32)]):
+                cells[0, mid, n : n + 1, :] = jnp.sum(
+                    jnp.where(at_cell, value, 0.0), axis=0, keepdims=True
+                )
+            for copy in cell_copies():
+                copy.start()
+
+        return copies
+
+    moving = cur_copies
     for step in range(STEPS):
         totals = bond_forces()
         load_near(step, 0)
         totals = add_forces(step, totals)
-        if step == 1:
-            for copy in post_copies:
-                copy.wait_recv()
-            g = stream(0)
-            density, inverse, velocity = moments(g)
-            store_post(1, collide(g, density, inverse, velocity))
-            post_copies = send_post(1)
-
-            @pl.when(is_mid)
-            def _():
-                for n, value in enumerate([density] + velocity + [row_ids.astype(F32)]):
-                    cells[0, mid, n : n + 1, :] = jnp.sum(
-                        jnp.where(at_cell, value, 0.0), axis=0, keepdims=True
-                    )
-                for copy in cell_copies():
-                    copy.start()
-
-        if step == 2:
-            for copy in post_copies:
-                copy.wait_recv()
-            g = stream(1)
-            for q in range(Q):
-                pop_out[q] = g[q]
         for k in (1, 2):
-            if step == 0:
-                cur_copies[k - 1].wait_recv()
-            else:
-                vel_copies[k - 1].wait_recv()
+            if step == 1 and k == 2:
+                post_copies = lattice_between()
+            moving[k - 1].wait_recv()
             if step == 1:
                 kick_copies[k - 1].wait_recv()
             load_near(step, k)
@@ -465,52 +472,60 @@
             speed = cur[0, 3 + axis]
             force = totals[axis] + (flow[axis : axis + 1] - DRAG_RATE * speed)
             speed = jnp.where(occupied, speed + TIME_STEP * force, 0.0)
-            place = cur[0, axis] + TIME_STEP * speed
             if last:
                 vel_out[axis] = speed
-                pos_out[axis] = jnp.where(occupied, place, 0.0)
-                sums[me_g, axis : axis + 1, :] = jnp.sum(speed, axis=0, keepdims=True)
+                sums[0, me_g, axis : axis + 1, :] = jnp.sum(speed, axis=0, keepdims=True)
             else:
                 cur[0, 3 + axis] = speed
-                cur[0, axis] = place
                 vel_send[step, axis] = speed
-        if last:
-            sums[me_g, 3:4, :] = count.astype(F32)
-        else:
-            vel_copies = [
-                send(
-                    vel_send.at[step],
-                    halo_vel.at[step, way],
-                    sem_vel.at[0, step, way],
-                    sem_vel.at[1, step, way],
-                    pair[way],
-                )
-                for way in range(2)
-            ]
-
-    for k in range(GROUPS - 1):
-        send(sums.at[me_g], sums.at[me_g], sem_sum.at[0, k], sem_sum.at[1, me_g], peers[k])
-    for k in range(GROUPS - 1):
-        other = peers[k][0]
-        remote(
-            sums.at[other], sums.at[other], sem_sum.at[0, k], sem_sum.at[1, other], peers[k]
-        ).wait_recv()
-    pooled = sums[0]
-    for n in range(1, GROUPS):
-        pooled = pooled + sums[n]
-    mean = pooled[0:3] / pooled[3:4]
+        if not last:
+            moving = send_pair(vel_send.at[step], halo_vel.at[step], sem_vel.at[step])
+            for axis in range(3):
+                cur[0, axis] += TIME_STEP * cur[0, 3 + axis]
+
+    sums[0, me_g, 3:4, :] = count.astype(F32)
+    for k in FARTHEST:
+        send(
+            sums.at[0, me_g], sums.at[0, me_g], sem_sum.at[k - 1], sem_sum.at[17 + me_g], peers[k - 1]
+        )
+    pl.semaphore_wait(sem_ready, len(far_mids))
+    for n in range(2):
+        send(sums.at[0, me_g], sums.at[1, me_g], sem_sum.at[15 + n], sem_sum.at[33 + me_g], far_mids[n])
+
+    for axis in range(3):
+        pos_out[axis] = jnp.where(occupied, cur[0, axis] + TIME_STEP * vel_out[axis], 0.0)
+    for copy in post_copies:
+        copy.wait_recv()
+    g = stream(1)
+    for q in range(Q):
+        pop_out[q] = g[q]
+
+    def wait_sums(which, others):
+        for other in others:
+            remote(
+                sums.at[which, other],
+                sums.at[which, other],
+                sem_sum.at[0],
+                sem_sum.at[17 + 16 * which + other],
+                peers[0],
+            ).wait_recv()
+
+    def pooled(which):
+        total = sums[which, 0]
+        for n in range(1, GROUPS):
+            total = total + sums[which, n]
+        return total[0:3] / total[3:4]
+
+    wait_sums(0, [peers[k - 1][0] for k in reversed(FARTHEST)])
+    mean = pooled(0)
     for axis in range(3):
         mean_out[axis] = mean[axis : axis + 1]
 
     @pl.when(is_mid)
     def _():
         means[2, 0:3] = mean
-        mean_copies = [
-            remote(means.at[2], means.at[1 - way], sem_mean.at[0, way], sem_mean.at[1, way], beside[way])
-            for way in range(2)
-        ]
-        for copy in mean_copies:
-            copy.start()
+        mean_copy = remote(means.at[2], means.at[0], sem_mean.at[0], sem_mean.at[1], pair[0])
+        mean_copy.start()
         for column in range(3):
             for n in range(2):
                 wait = remote(
@@ -554,17 +569,17 @@
                 pop_out[q] += tile
 
         change(0, mean, [q for q in range(Q) if VELOCITY_SET[q][0] == 0])
-        for way in range(2):
-            mean_copies[way].wait_recv()
-            change(2 - way, means[1 - way], TO_BRICK[way])
-        for copy in mean_copies:
-            copy.wait_send()
+        mean_copy.wait_recv()
+        wait_sums(1, range(GROUPS))
+        far_mean = pooled(1)
+        near_mean = means[0, 0:3]
+        change(1, jnp.where(even, near_mean, far_mean), TO_BRICK[1])
+        change(2, jnp.where(even, far_mean, near_mean), TO_BRICK[0])
+        mean_copy.wait_send()
         for copy in cell_copies():
             copy.wait_send()
-        for k in range(GROUPS - 1):
-            remote(
-                drag.at[mid], drag.at[mid], sem_drag.at[k], sem_drag.at[16 + mid], peers[k]
-            ).wait_send()
+        for copy in drag_copies():
+            copy.wait_send()
 
     for copy in unsent:
         if not any(copy is other for other in cur_copies):
@@ -623,7 +638,7 @@
             pltpu.VMEM((2, 2, 5, 1, NZ), F32),
             pltpu.VMEM((2, 2, 5, 1, NZ), F32),
             pltpu.VMEM((3, 2, 8, NZ), F32),
-            pltpu.VMEM((GROUPS, 4, NZ), F32),
+            pltpu.VMEM((2, GROUPS, 4, NZ), F32),
             pltpu.VMEM((3, 8, NZ), F32),
             dma((2, 2)),
             dma((2, 2)),
@@ -632,8 +647,10 @@
             dma((2, 2, 2)),
             dma((2, 2, 2, 3)),
             dma((11,)),
-            dma((2, GROUPS)),
-            dma((2, 2)),
+            dma((49,)),
+            dma((2,)),
+            pltpu.SemaphoreType.REGULAR,
+            pltpu.SemaphoreType.REGULAR,
         ],
         compiler_params=pltpu.CompilerParams(
             collective_id=0, has_side_effects=True, vmem_limit_bytes=4 << 20

time: 39.3 us -> 38.1 us (0.969)
  Pallas kernels: 38.5 us -> 37.3 us
    pallas_call x1, Pallas kernels: 37.9 us -> 36.6 us  [local(): pl.pallas_call(kernel, out_shape=(pltpu.VMEM((Q, LY, NZ), F32), pltpu.VME...]
where the time goes in v3:
time: 38.1 us; the launch traced here: 37.9 us
  Pallas kernels  37.3 us (98%)
  between operations  0.64 us (2%)
    pallas_call x1, Pallas kernels, local(): pl.pallas_call(kernel, out_shape=(pltpu.VMEM((Q, LY, NZ), F32), pltpu.VME...  36.6 us

profile of v3, /device:TPU:88, one launch (start us, length us, event | category | flops | bytes accessed | tf_op | source)
XLA Modules:
  0.0 37.9 jit_solution(15582750630644510585)
XLA Ops:
  0.6 36.6 %cycle.1 = (f32[19,8,128]{2,1,0:T(8,128)S(1)}, f32[3,1,128]{2,1,0:T(1,128)S(1)}, f32[3,16,128]{2,1,0:T(8,128)S(1)}, f32[3,16,128]{2,1,0:T(8,128)S(1)}) custom-call(f32[19,8,128]{2,1,0:T(8,128)} %bitcast.16, s32[1,128]{1,0:T(1,128)} %rows_hbm.1, f32[3,16,128]{2,1,0:T(8,128)} %bitcast.17, f32[3,16,128]{2,1,0:T(8,128)} %bitcast.18, f32[3,16,128]{2,1,0:T(8,128)} %bitcast.19, ...), custom_call_target="tpu_custom_call" | custom-call | tf_op jit(solution)/shard_map/cycle/pallas_call | solution.py:609
  37.2 0.7 %hand_out.1 = (f32[19,8,128]{2,1,0:T(8,128)}, f32[3,1,128]{2,1,0:T(1,128)}, f32[3,16,128]{2,1,0:T(8,128)}, f32[3,16,128]{2,1,0:T(8,128)}) custom-call(f32[19,8,128]{2,1,0:T(8,128)S(1)} %get-tuple-element.12.refs_0_, f32[3,1,128]{2,1,0:T(1,128)S(1)} %get-tuple-element.13.refs_1_, f32[3,16,128]{2,1,0:T(8,128)S(1)} %get-tuple-element.14.refs_2_, ...), custom_call_target="tpu_custom_call" | custom-call | tf_op jit(solution)/shard_map/hand_out/pallas_call | solution.py:674

commit v4 on v3

--- a/solution.py
+++ b/solution.py
@@ -165,6 +165,9 @@
 
     far_mids = [(MIDDLE, pair[1][1]), (MIDDLE + 1, pair[1][1])]
 
+    barrier = pltpu.get_barrier_semaphore()
+    pl.semaphore_signal(barrier, inc=1, device_id=pair[1], device_id_type=MESH)
+
     loads = {}
     for n, (name, source, target) in enumerate(
         (
@@ -181,9 +184,8 @@
         loads[name] = pltpu.make_async_copy(source, target, sem_in.at[n])
         loads[name].start()
 
-    barrier = pltpu.get_barrier_semaphore()
     partners = pair[::-1] + [peers[k - 1] for k in FARTHEST] + corners
-    for device in partners:
+    for device in partners[1:]:
         pl.semaphore_signal(barrier, inc=1, device_id=device, device_id_type=MESH)
 
     unsent = []
@@ -211,13 +213,15 @@
     occupied = slot_ids < count
     tails = type_in[...].astype(F32)
     own_tail = type_in[...] == 1
-    cur[0, 0] = jnp.where(occupied, pos_in[0], FAR)
-    cur[0, 1] = pos_in[1]
-    cur[0, 2] = pos_in[2]
-    for axis in range(3):
-        cur[0, 3 + axis] = vel_in[axis]
-    cur[0, 6] = kick_in[0]
-    cur[0, 7] = tails
+    for c in range(2):
+        half = slice(8 * c, 8 * c + 8)
+        cur[0, c, 0] = jnp.where(occupied[half], pos_in[0, half], FAR)
+        for axis in range(1, 3):
+            cur[0, c, axis] = pos_in[axis, half]
+        for axis in range(3):
+            cur[0, c, 3 + axis] = vel_in[axis, half]
+        cur[0, c, 6] = kick_in[0, half]
+        cur[0, c, 7] = tails[half]
 
     pl.semaphore_wait(barrier, len(partners))
 
@@ -225,14 +229,15 @@
     def _():
         pl.semaphore_signal(sem_entered, inc=1, device_id=pair[1], device_id_type=MESH)
 
-    def send_pair(source, target, sems):
-        copies = [
-            send(source, target.at[way], sems.at[0, way], sems.at[1, way], pair[way])
-            for way in (1, 0)
-        ]
-        return copies[::-1]
-
-    cur_copies = send_pair(cur.at[0], cur.at[pl.ds(1, 2)], sem_cur)
+    def send_near(source, target, sems):
+        return send(source, target, sems.at[0, 0], sems.at[1, 0], pair[0])
+
+    def send_far(source, target, sems, c):
+        return send(source, target, sems.at[0, 1 + c], sems.at[1, 1 + c], pair[1])
+
+    far_copies = [send_far(cur.at[0, c], cur.at[2, c], sem_cur, c) for c in range(2)]
+    near_copy = send_near(cur.at[0], cur.at[1], sem_cur)
+    cur_copies = far_copies + [near_copy]
 
     row_ids = me_g * LY + lax.broadcasted_iota(jnp.int32, (LY, NZ), 0)
     first_row = lax.broadcasted_iota(jnp.int32, (LY, NZ), 0) == 0
@@ -261,7 +266,10 @@
         for copy in drag_copies():
             copy.start()
 
-    kick_copies = send_pair(kick_in.at[pl.ds(1, 2)], halo_kick, sem_kick)
+    kick_copies = [
+        send(kick_in.at[pl.ds(1, 2)], halo_kick.at[way], sem_kick.at[0, way], sem_kick.at[1, way], pair[way])
+        for way in range(2)
+    ]
 
     def store_post(stage, values):
         for q in range(Q):
@@ -326,24 +334,25 @@
 
     post_copies = send_post(0)
 
-    def load_near(step, k):
+    def load_near(step, k, c):
+        half = slice(8 * c, 8 * c + 8)
         shift = (0.0, side, -side)[k]
-        places = [cur[k, axis] for axis in range(3)]
+        places = [cur[k, c, axis] for axis in range(3)]
         if k == 0 or step == 0:
-            speeds = [cur[k, 3 + axis] for axis in range(3)]
+            speeds = [cur[k, c, 3 + axis] for axis in range(3)]
         else:
-            speeds = [halo_vel[step - 1, k - 1, axis] for axis in range(3)]
+            speeds = [halo_vel[step - 1, k - 1, c, axis] for axis in range(3)]
             places = [p + TIME_STEP * v for p, v in zip(places, speeds)]
             if step < STEPS - 1:
                 for axis in range(3):
-                    cur[k, axis] = places[axis]
+                    cur[k, c, axis] = places[axis]
         if step == 0:
-            kick = cur[k, 6]
+            kick = cur[k, c, 6]
         elif k == 0:
-            kick = kick_in[step]
+            kick = kick_in[step, half]
         else:
-            kick = halo_kick[k - 1, step - 1]
-        tail = cur[k, 7]
+            kick = halo_kick[k - 1, step - 1, half]
+        tail = cur[k, c, 7]
         push = KICK_SCALE * kick
         fields = [
             places[0] + shift,
@@ -361,44 +370,41 @@
                     field = pltpu.roll(field, (-b) % NZ, 1)
                 if f == 2:
                     field = field + float(b)
-                near[n, f] = field
-
-    def add_forces(step, totals):
-        xi, yi, zi = [cur[0, axis] for axis in range(3)]
-        ui, vi, wi = [FRICTION * cur[0, 3 + axis] for axis in range(3)]
-        ki = KICK_SCALE * kick_in[step]
-
-        def tile(n, totals):
-            fx, fy, fz = totals
-            for j in range(CAP):
-                xj, yj, zj, uj, vj, wj, a0, a1 = [near[n, f, j : j + 1, :] for f in range(8)]
+                near[c, n, f] = field
+
+    def add_forces(step, c, own, totals):
+        half = slice(8 * own, 8 * own + 8)
+        xi, yi, zi = [cur[0, own, axis] for axis in range(3)]
+        ui, vi, wi = [FRICTION * cur[0, own, 3 + axis] for axis in range(3)]
+        ki = KICK_SCALE * kick_in[step, half]
+        tail = own_tail[half]
+        fx, fy, fz = totals
+        for n in range(3):
+            for j in range(8):
+                xj, yj, zj, uj, vj, wj, a0, a1 = [near[c, n, f, j : j + 1, :] for f in range(8)]
                 dx = xi - xj
                 dy = yi - yj
                 dz = zi - zj
                 weight = jnp.maximum(1.0 - (dx * dx + dy * dy + dz * dz), 0.0)
                 closing = dx * (ui - uj) + dy * (vi - vj) + dz * (wi - wj)
-                lift = jnp.where(own_tail, a1, a0) + ki
+                lift = jnp.where(tail, a1, a0) + ki
                 strength = weight * (lift - weight * closing)
                 fx = fx + strength * dx
                 fy = fy + strength * dy
                 fz = fz + strength * dz
-            return fx, fy, fz
-
-        for n in range(3):
-            totals = tile(n, totals)
-        return totals
+        return fx, fy, fz
 
     loads["partner"].wait()
     partner = partner_in[...]
     partner = jnp.where(partner < count, partner, slot_ids)
 
-    def bond_forces():
-        places = [cur[0, axis] for axis in range(3)]
+    def bond_forces(own):
+        places = [cur[0, own, axis] for axis in range(3)]
         found = list(places)
         for j in range(CAP):
-            match = partner == j
+            match = partner[8 * own : 8 * own + 8] == j
             for axis in range(3):
-                found[axis] = jnp.where(match, cur[0, axis, j : j + 1, :], found[axis])
+                found[axis] = jnp.where(match, cur[0, j // 8, axis, j % 8 : j % 8 + 1, :], found[axis])
         return tuple(-BOND_STIFF * (p - f) for p, f in zip(places, found))
 
     def cell_copies():
@@ -442,81 +448,103 @@
 
         return copies
 
-    moving = cur_copies
+    def advance(step, own, totals):
+        half = slice(8 * own, 8 * own + 8)
+        for axis in range(3):
+            speed = cur[0, own, 3 + axis]
+            force = totals[axis] + (flow[axis : axis + 1] - DRAG_RATE * speed)
+            speed = jnp.where(occupied[half], speed + TIME_STEP * force, 0.0)
+            cur[0, own, 3 + axis] = speed
+            if step < STEPS - 1:
+                vel_send[step, own, axis] = speed
+            else:
+                vel_out[axis, half] = speed
+
     for step in range(STEPS):
-        totals = bond_forces()
-        load_near(step, 0)
-        totals = add_forces(step, totals)
-        for k in (1, 2):
+        totals = [bond_forces(own) for own in range(2)]
+        for k in range(3):
             if step == 1 and k == 2:
                 post_copies = lattice_between()
-            moving[k - 1].wait_recv()
-            if step == 1:
+            if k == 1:
+                near_copy.wait_recv()
+            if step == 1 and k:
                 kick_copies[k - 1].wait_recv()
-            load_near(step, k)
-            totals = add_forces(step, totals)
-        if step == 0:
-            for n in range(2):
-
-                @pl.when(me_g != MIDDLE + n)
-                def _():
-                    remote(
-                        drag.at[n], drag.at[n], sem_drag.at[0], sem_drag.at[16 + n], peers[0]
-                    ).wait_recv()
-
-            flow = (DRAG_RATE / VELOCITY_SCALE) * (drag[0, 0:3] + drag[1, 0:3])
-            for copy in cur_copies:
-                copy.wait_send()
-        last = step == STEPS - 1
-        for axis in range(3):
-            speed = cur[0, 3 + axis]
-            force = totals[axis] + (flow[axis : axis + 1] - DRAG_RATE * speed)
-            speed = jnp.where(occupied, speed + TIME_STEP * force, 0.0)
-            if last:
-                vel_out[axis] = speed
-                sums[0, me_g, axis : axis + 1, :] = jnp.sum(speed, axis=0, keepdims=True)
-            else:
-                cur[0, 3 + axis] = speed
-                vel_send[step, axis] = speed
-        if not last:
-            moving = send_pair(vel_send.at[step], halo_vel.at[step], sem_vel.at[step])
-            for axis in range(3):
-                cur[0, axis] += TIME_STEP * cur[0, 3 + axis]
-
-    sums[0, me_g, 3:4, :] = count.astype(F32)
+            for c in range(2):
+                if k == 2:
+                    far_copies[c].wait_recv()
+                load_near(step, k, c)
+                if step == 0 and k == 2 and c == 1:
+                    for n in range(2):
+
+                        @pl.when(me_g != MIDDLE + n)
+                        def _():
+                            remote(
+                                drag.at[n], drag.at[n], sem_drag.at[0], sem_drag.at[16 + n], peers[0]
+                            ).wait_recv()
+
+                    flow = (DRAG_RATE / VELOCITY_SCALE) * (drag[0, 0:3] + drag[1, 0:3])
+                    for copy in cur_copies:
+                        copy.wait_send()
+                sent = []
+                for own in range(2):
+                    totals[own] = add_forces(step, c, own, totals[own])
+                    if k == 2 and c == 1:
+                        advance(step, own, totals[own])
+                        if step < STEPS - 1:
+                            sent.append(
+                                send_far(
+                                    vel_send.at[step, own],
+                                    halo_vel.at[step, 1, own],
+                                    sem_vel.at[step],
+                                    own,
+                                )
+                            )
+        if step < STEPS - 1:
+            far_copies = sent
+            near_copy = send_near(vel_send.at[step], halo_vel.at[step, 0], sem_vel.at[step])
+            for own in range(2):
+                for axis in range(3):
+                    cur[0, own, axis] += TIME_STEP * cur[0, own, 3 + axis]
+
+    for axis in range(3):
+        sums[me_g, axis : axis + 1, :] = jnp.sum(
+            cur[0, 0, 3 + axis] + cur[0, 1, 3 + axis], axis=0, keepdims=True
+        )
+    sums[me_g, 3:4, :] = count.astype(F32)
     for k in FARTHEST:
-        send(
-            sums.at[0, me_g], sums.at[0, me_g], sem_sum.at[k - 1], sem_sum.at[17 + me_g], peers[k - 1]
-        )
+        remote(sums.at[me_g], sums.at[me_g], sem_sum.at[0], sem_sum.at[1], peers[k - 1]).start()
     pl.semaphore_wait(sem_ready, len(far_mids))
     for n in range(2):
-        send(sums.at[0, me_g], sums.at[1, me_g], sem_sum.at[15 + n], sem_sum.at[33 + me_g], far_mids[n])
+        remote(
+            sums.at[me_g], sums.at[GROUPS + me_g], sem_sum.at[0], sem_sum.at[2], far_mids[n]
+        ).start()
+
+    def all_sums(start, size, recv_sem):
+        part = sums.at[pl.ds(start, size)]
+        return remote(part, part, sem_sum.at[0], recv_sem, peers[0])
 
     for axis in range(3):
-        pos_out[axis] = jnp.where(occupied, cur[0, axis] + TIME_STEP * vel_out[axis], 0.0)
+        for own in range(2):
+            half = slice(8 * own, 8 * own + 8)
+            place = cur[0, own, axis] + TIME_STEP * cur[0, own, 3 + axis]
+            pos_out[axis, half] = jnp.where(occupied[half], place, 0.0)
     for copy in post_copies:
         copy.wait_recv()
     g = stream(1)
     for q in range(Q):
         pop_out[q] = g[q]
 
-    def wait_sums(which, others):
-        for other in others:
-            remote(
-                sums.at[which, other],
-                sums.at[which, other],
-                sem_sum.at[0],
-                sem_sum.at[17 + 16 * which + other],
-                peers[0],
-            ).wait_recv()
+    for copy in unsent:
+        if not any(copy is other for other in cur_copies):
+            copy.wait_send()
 
     def pooled(which):
-        total = sums[which, 0]
+        total = sums[GROUPS * which]
         for n in range(1, GROUPS):
-            total = total + sums[which, n]
+            total = total + sums[GROUPS * which + n]
         return total[0:3] / total[3:4]
 
-    wait_sums(0, [peers[k - 1][0] for k in reversed(FARTHEST)])
+    all_sums(0, GROUPS - 1, sem_sum.at[1]).wait_recv()
     mean = pooled(0)
     for axis in range(3):
         mean_out[axis] = mean[axis : axis + 1]
@@ -570,7 +598,7 @@
 
         change(0, mean, [q for q in range(Q) if VELOCITY_SET[q][0] == 0])
         mean_copy.wait_recv()
-        wait_sums(1, range(GROUPS))
+        all_sums(GROUPS, GROUPS, sem_sum.at[2]).wait_recv()
         far_mean = pooled(1)
         near_mean = means[0, 0:3]
         change(1, jnp.where(even, near_mean, far_mean), TO_BRICK[1])
@@ -581,9 +609,7 @@
         for copy in drag_copies():
             copy.wait_send()
 
-    for copy in unsent:
-        if not any(copy is other for other in cur_copies):
-            copy.wait_send()
+    all_sums(0, GROUPS + 1, sem_sum.at[1]).wait_send()
 
 
 def hand_out(*refs):
@@ -626,28 +652,28 @@
             pltpu.VMEM(bead, jnp.int32),
             pltpu.VMEM((1, NZ), jnp.int32),
             dma((8,)),
-            pltpu.VMEM((3, 8, *bead), F32),
+            pltpu.VMEM((3, 2, 8, 8, NZ), F32),
             pltpu.VMEM((2, 2, *bead), F32),
-            pltpu.VMEM((2, 3, *bead), F32),
-            pltpu.VMEM((2, 2, 3, *bead), F32),
-            pltpu.VMEM((3, 8, *bead), F32),
-            pltpu.VMEM((2, 8, NZ), F32),
+            pltpu.VMEM((2, 2, 3, 8, NZ), F32),
+            pltpu.VMEM((2, 2, 2, 3, 8, NZ), F32),
+            pltpu.VMEM((2, 3, 8, 8, NZ), F32),
+            pltpu.VMEM((2, 4, NZ), F32),
             pltpu.VMEM((2, Q, LY, NZ), F32),
             pltpu.VMEM((2, 2, 5, LY, NZ), F32),
             pltpu.VMEM((2, 2, 5, LY, NZ), F32),
             pltpu.VMEM((2, 2, 5, 1, NZ), F32),
             pltpu.VMEM((2, 2, 5, 1, NZ), F32),
             pltpu.VMEM((3, 2, 8, NZ), F32),
-            pltpu.VMEM((2, GROUPS, 4, NZ), F32),
+            pltpu.VMEM((2 * GROUPS, 4, NZ), F32),
             pltpu.VMEM((3, 8, NZ), F32),
+            dma((2, 3)),
             dma((2, 2)),
-            dma((2, 2)),
-            dma((2, 2, 2)),
+            dma((2, 2, 3)),
             dma((18,)),
             dma((2, 2, 2)),
             dma((2, 2, 2, 3)),
             dma((11,)),
-            dma((49,)),
+            dma((3,)),
             dma((2,)),
             pltpu.SemaphoreType.REGULAR,
             pltpu.SemaphoreType.REGULAR,

time: 38.1 us -> 37 us (0.971)
  Pallas kernels: 37.3 us -> 36.2 us
    pallas_call x1, Pallas kernels: 36.6 us -> 35.6 us  [local(): pl.pallas_call(kernel, out_shape=(pltpu.VMEM((Q, LY, NZ), F32), pltpu.VME...]
where the time goes in v4:
time: 37 us; the launch traced here: 36.9 us
  Pallas kernels  36.2 us (98%)
  between operations  0.64 us (2%)
    pallas_call x1, Pallas kernels, local(): pl.pallas_call(kernel, out_shape=(pltpu.VMEM((Q, LY, NZ), F32), pltpu.VME...  35.6 us

profile of v4, /device:TPU:88, one launch (start us, length us, event | category | flops | bytes accessed | tf_op | source)
XLA Modules:
  0.0 36.9 jit_solution(7359763951246310993)
XLA Ops:
  0.6 35.6 %cycle.1 = (f32[19,8,128]{2,1,0:T(8,128)S(1)}, f32[3,1,128]{2,1,0:T(1,128)S(1)}, f32[3,16,128]{2,1,0:T(8,128)S(1)}, f32[3,16,128]{2,1,0:T(8,128)S(1)}) custom-call(f32[19,8,128]{2,1,0:T(8,128)} %bitcast.16, s32[1,128]{1,0:T(1,128)} %rows_hbm.1, f32[3,16,128]{2,1,0:T(8,128)} %bitcast.17, f32[3,16,128]{2,1,0:T(8,128)} %bitcast.18, f32[3,16,128]{2,1,0:T(8,128)} %bitcast.19, ...), custom_call_target="tpu_custom_call" | custom-call | tf_op jit(solution)/shard_map/cycle/pallas_call | solution.py:635
  36.2 0.7 %hand_out.1 = (f32[19,8,128]{2,1,0:T(8,128)}, f32[3,1,128]{2,1,0:T(1,128)}, f32[3,16,128]{2,1,0:T(8,128)}, f32[3,16,128]{2,1,0:T(8,128)}) custom-call(f32[19,8,128]{2,1,0:T(8,128)S(1)} %get-tuple-element.12.refs_0_, f32[3,1,128]{2,1,0:T(1,128)S(1)} %get-tuple-element.13.refs_1_, f32[3,16,128]{2,1,0:T(8,128)S(1)} %get-tuple-element.14.refs_2_, ...), custom_call_target="tpu_custom_call" | custom-call | tf_op jit(solution)/shard_map/hand_out/pallas_call | solution.py:700

commit v5 on v4

--- a/solution.py
+++ b/solution.py
@@ -147,6 +147,7 @@
     sem_mean,
     sem_entered,
     sem_ready,
+    sem_corner,
 ):
     me_g = lax.axis_index("group")
     me_b = lax.axis_index("brick")
@@ -161,7 +162,6 @@
     even = lax.rem(me_b, 2) == 0
     pair = [(me_g, jnp.where(even, up_b, dn_b)), (me_g, jnp.where(even, dn_b, up_b))]
     side = jnp.where(even, 1.0, -1.0)
-    corners = [(up_g, up_b), (up_g, dn_b), (dn_g, up_b), (dn_g, dn_b)]
 
     far_mids = [(MIDDLE, pair[1][1]), (MIDDLE + 1, pair[1][1])]
 
@@ -184,9 +184,17 @@
         loads[name] = pltpu.make_async_copy(source, target, sem_in.at[n])
         loads[name].start()
 
-    partners = pair[::-1] + [peers[k - 1] for k in FARTHEST] + corners
-    for device in partners[1:]:
-        pl.semaphore_signal(barrier, inc=1, device_id=device, device_id_type=MESH)
+    pl.semaphore_signal(barrier, inc=1, device_id=pair[0], device_id_type=MESH)
+    for n in range(2):
+
+        @pl.when(me_g != MIDDLE + n)
+        def _():
+            pl.semaphore_signal(
+                barrier, inc=1, device_id=(MIDDLE + n, me_b), device_id_type=MESH
+            )
+
+    for group in (up_g, dn_g):
+        pl.semaphore_signal(barrier, inc=1, device_id=(group, me_b), device_id_type=MESH)
 
     unsent = []
 
@@ -223,21 +231,24 @@
         cur[0, c, 6] = kick_in[0, half]
         cur[0, c, 7] = tails[half]
 
-    pl.semaphore_wait(barrier, len(partners))
+    pl.semaphore_wait(barrier, jnp.where(is_mid, 4 + GROUPS - 1, 4))
+
+    def send_near(source, target, sems):
+        return send(source, target, sems.at[0, 0], sems.at[1, 0], pair[0])
+
+    def send_far(source, target, sems, c):
+        return send(source, target, sems.at[0, 1 + c], sems.at[1, 1 + c], pair[1])
+
+    far_copies = [send_far(cur.at[0, c], cur.at[2, c], sem_cur, c) for c in range(2)]
+    near_copy = send_near(cur.at[0], cur.at[1], sem_cur)
+    cur_copies = far_copies + [near_copy]
+
+    for group in (up_g, dn_g):
+        pl.semaphore_signal(sem_corner, inc=1, device_id=(group, me_b), device_id_type=MESH)
 
     @pl.when(is_mid)
     def _():
         pl.semaphore_signal(sem_entered, inc=1, device_id=pair[1], device_id_type=MESH)
-
-    def send_near(source, target, sems):
-        return send(source, target, sems.at[0, 0], sems.at[1, 0], pair[0])
-
-    def send_far(source, target, sems, c):
-        return send(source, target, sems.at[0, 1 + c], sems.at[1, 1 + c], pair[1])
-
-    far_copies = [send_far(cur.at[0, c], cur.at[2, c], sem_cur, c) for c in range(2)]
-    near_copy = send_near(cur.at[0], cur.at[1], sem_cur)
-    cur_copies = far_copies + [near_copy]
 
     row_ids = me_g * LY + lax.broadcasted_iota(jnp.int32, (LY, NZ), 0)
     first_row = lax.broadcasted_iota(jnp.int32, (LY, NZ), 0) == 0
@@ -331,8 +342,6 @@
                 )
             moved.append(value)
         return moved
-
-    post_copies = send_post(0)
 
     def load_near(step, k, c):
         half = slice(8 * c, 8 * c + 8)
@@ -460,9 +469,25 @@
             else:
                 vel_out[axis, half] = speed
 
+    def wait_drag():
+        for n in range(2):
+
+            @pl.when(me_g != MIDDLE + n)
+            def _():
+                remote(
+                    drag.at[n], drag.at[n], sem_drag.at[0], sem_drag.at[16 + n], peers[0]
+                ).wait_recv()
+
+        for copy in cur_copies:
+            copy.wait_send()
+        return (DRAG_RATE / VELOCITY_SCALE) * (drag[0, 0:3] + drag[1, 0:3])
+
     for step in range(STEPS):
         totals = [bond_forces(own) for own in range(2)]
         for k in range(3):
+            if step == 0 and k == 2:
+                pl.semaphore_wait(sem_corner, 2)
+                post_copies = send_post(0)
             if step == 1 and k == 2:
                 post_copies = lattice_between()
             if k == 1:
@@ -473,22 +498,12 @@
                 if k == 2:
                     far_copies[c].wait_recv()
                 load_near(step, k, c)
-                if step == 0 and k == 2 and c == 1:
-                    for n in range(2):
-
-                        @pl.when(me_g != MIDDLE + n)
-                        def _():
-                            remote(
-                                drag.at[n], drag.at[n], sem_drag.at[0], sem_drag.at[16 + n], peers[0]
-                            ).wait_recv()
-
-                    flow = (DRAG_RATE / VELOCITY_SCALE) * (drag[0, 0:3] + drag[1, 0:3])
-                    for copy in cur_copies:
-                        copy.wait_send()
                 sent = []
                 for own in range(2):
                     totals[own] = add_forces(step, c, own, totals[own])
                     if k == 2 and c == 1:
+                        if step == 0 and own == 0:
+                            flow = wait_drag()
                         advance(step, own, totals[own])
                         if step < STEPS - 1:
                             sent.append(
@@ -677,6 +692,7 @@
             dma((2,)),
             pltpu.SemaphoreType.REGULAR,
             pltpu.SemaphoreType.REGULAR,
+            pltpu.SemaphoreType.REGULAR,
         ],
         compiler_params=pltpu.CompilerParams(
             collective_id=0, has_side_effects=True, vmem_limit_bytes=4 << 20

time: 37 us -> 35.3 us (0.954)
  the two profiles are of different devices: /device:TPU:88 before, /device:TPU:33 now
where the time goes in v5:
time: 35.3 us; the launch traced here: 35.1 us
  Pallas kernels  34.5 us (98%)
  between operations  0.64 us (2%)
    pallas_call x1, Pallas kernels, local(): pl.pallas_call(kernel, out_shape=(pltpu.VMEM((Q, LY, NZ), F32), pltpu.VME...  33.8 us

profile of v5, /device:TPU:33, one launch (start us, length us, event | category | flops | bytes accessed | tf_op | source)
XLA Modules:
  0.0 35.1 jit_solution(5483230973877738380)
XLA Ops:
  0.6 33.8 %cycle.1 = (f32[19,8,128]{2,1,0:T(8,128)S(1)}, f32[3,1,128]{2,1,0:T(1,128)S(1)}, f32[3,16,128]{2,1,0:T(8,128)S(1)}, f32[3,16,128]{2,1,0:T(8,128)S(1)}) custom-call(f32[19,8,128]{2,1,0:T(8,128)} %bitcast.16, s32[1,128]{1,0:T(1,128)} %rows_hbm.1, f32[3,16,128]{2,1,0:T(8,128)} %bitcast.17, f32[3,16,128]{2,1,0:T(8,128)} %bitcast.18, f32[3,16,128]{2,1,0:T(8,128)} %bitcast.19, ...), custom_call_target="tpu_custom_call" | custom-call | tf_op jit(solution)/shard_map/cycle/pallas_call | solution.py:650
  34.4 0.7 %hand_out.1 = (f32[19,8,128]{2,1,0:T(8,128)}, f32[3,1,128]{2,1,0:T(1,128)}, f32[3,16,128]{2,1,0:T(8,128)}, f32[3,16,128]{2,1,0:T(8,128)}) custom-call(f32[19,8,128]{2,1,0:T(8,128)S(1)} %get-tuple-element.12.refs_0_, f32[3,1,128]{2,1,0:T(1,128)S(1)} %get-tuple-element.13.refs_1_, f32[3,16,128]{2,1,0:T(8,128)S(1)} %get-tuple-element.14.refs_2_, ...), custom_call_target="tpu_custom_call" | custom-call | tf_op jit(solution)/shard_map/hand_out/pallas_call | solution.py:716

commit v6 on v5

--- a/solution.py
+++ b/solution.py
@@ -123,6 +123,7 @@
     count_in,
     sem_in,
     cur,
+    partners,
     halo_kick,
     vel_send,
     halo_vel,
@@ -137,6 +138,7 @@
     sums,
     means,
     sem_cur,
+    sem_partner,
     sem_kick,
     sem_vel,
     sem_drag,
@@ -145,8 +147,6 @@
     sem_cell,
     sem_sum,
     sem_mean,
-    sem_entered,
-    sem_ready,
     sem_corner,
 ):
     me_g = lax.axis_index("group")
@@ -162,6 +162,9 @@
     even = lax.rem(me_b, 2) == 0
     pair = [(me_g, jnp.where(even, up_b, dn_b)), (me_g, jnp.where(even, dn_b, up_b))]
     side = jnp.where(even, 1.0, -1.0)
+    ahead2 = (me_g, lax.rem(me_b + jnp.where(even, 2, BRICKS - 2), BRICKS))
+    back2 = (me_g, lax.rem(me_b + jnp.where(even, BRICKS - 2, 2), BRICKS))
+    targets = [pair[0], pair[1], ahead2]
 
     far_mids = [(MIDDLE, pair[1][1]), (MIDDLE + 1, pair[1][1])]
 
@@ -184,8 +187,10 @@
         loads[name] = pltpu.make_async_copy(source, target, sem_in.at[n])
         loads[name].start()
 
-    pl.semaphore_signal(barrier, inc=1, device_id=pair[0], device_id_type=MESH)
+    for device in (pair[0], back2):
+        pl.semaphore_signal(barrier, inc=1, device_id=device, device_id_type=MESH)
     for n in range(2):
+        pl.semaphore_signal(barrier, inc=1, device_id=far_mids[n], device_id_type=MESH)
 
         @pl.when(me_g != MIDDLE + n)
         def _():
@@ -214,13 +219,14 @@
         unsent.append(copy)
         return copy
 
-    for name in ("pos", "vel", "kick", "type", "count"):
+    for name in ("pos", "vel", "kick", "type", "count", "partner"):
         loads[name].wait()
     slot_ids = lax.broadcasted_iota(jnp.int32, (CAP, NZ), 0)
     count = count_in[...]
     occupied = slot_ids < count
     tails = type_in[...].astype(F32)
-    own_tail = type_in[...] == 1
+    partner = partner_in[...]
+    partners[0] = jnp.where(partner < count, partner, slot_ids)
     for c in range(2):
         half = slice(8 * c, 8 * c + 8)
         cur[0, c, 0] = jnp.where(occupied[half], pos_in[0, half], FAR)
@@ -231,24 +237,19 @@
         cur[0, c, 6] = kick_in[0, half]
         cur[0, c, 7] = tails[half]
 
-    pl.semaphore_wait(barrier, jnp.where(is_mid, 4 + GROUPS - 1, 4))
-
-    def send_near(source, target, sems):
-        return send(source, target, sems.at[0, 0], sems.at[1, 0], pair[0])
-
-    def send_far(source, target, sems, c):
-        return send(source, target, sems.at[0, 1 + c], sems.at[1, 1 + c], pair[1])
-
-    far_copies = [send_far(cur.at[0, c], cur.at[2, c], sem_cur, c) for c in range(2)]
-    near_copy = send_near(cur.at[0], cur.at[1], sem_cur)
-    cur_copies = far_copies + [near_copy]
+    pl.semaphore_wait(barrier, jnp.where(is_mid, 5 + 2 * GROUPS - 1, 5))
+
+    def spread(source, target, sems, which):
+        return {
+            k: send(source, target.at[k], sems.at[0, k - 1], sems.at[1, k - 1], targets[k - 1])
+            for k in which
+        }
+
+    cur_copies = spread(cur.at[0], cur, sem_cur, (2, 3, 1))
+    partner_copies = spread(partners.at[0], partners, sem_partner, (2,))
 
     for group in (up_g, dn_g):
         pl.semaphore_signal(sem_corner, inc=1, device_id=(group, me_b), device_id_type=MESH)
-
-    @pl.when(is_mid)
-    def _():
-        pl.semaphore_signal(sem_entered, inc=1, device_id=pair[1], device_id_type=MESH)
 
     row_ids = me_g * LY + lax.broadcasted_iota(jnp.int32, (LY, NZ), 0)
     first_row = lax.broadcasted_iota(jnp.int32, (LY, NZ), 0) == 0
@@ -263,24 +264,28 @@
     density, inverse, velocity = moments(g)
 
     def drag_copies():
-        return [
-            remote(drag.at[mid], drag.at[mid], sem_drag.at[k - 1], sem_drag.at[16 + mid], peers[k - 1])
+        copies = [
+            remote(drag.at[0, mid], drag.at[0, mid], sem_drag.at[15 + k], sem_drag.at[31 + mid], peers[k - 1])
             for k in FARTHEST
+        ]
+        return copies + [
+            remote(drag.at[0, mid], drag.at[1, mid], sem_drag.at[n], sem_drag.at[33 + mid], (n, pair[1][1]))
+            for n in range(GROUPS)
         ]
 
     @pl.when(is_mid)
     def _():
         for axis in range(3):
-            drag[mid, axis : axis + 1, :] = jnp.sum(
+            drag[0, mid, axis : axis + 1, :] = jnp.sum(
                 jnp.where(at_cell, velocity[axis], 0.0), axis=0, keepdims=True
             )
         for copy in drag_copies():
             copy.start()
 
-    kick_copies = [
-        send(kick_in.at[pl.ds(1, 2)], halo_kick.at[way], sem_kick.at[0, way], sem_kick.at[1, way], pair[way])
-        for way in range(2)
-    ]
+    kick_copies = spread(kick_in.at[pl.ds(1, 2)], halo_kick, sem_kick, (2, 1))
+    kick_copies[3] = send(
+        kick_in.at[1], halo_kick.at[3, 0], sem_kick.at[0, 2], sem_kick.at[1, 2], ahead2
+    )
 
     def store_post(stage, values):
         for q in range(Q):
@@ -343,78 +348,109 @@
             moved.append(value)
         return moved
 
-    def load_near(step, k, c):
-        half = slice(8 * c, 8 * c + 8)
-        shift = (0.0, side, -side)[k]
-        places = [cur[k, c, axis] for axis in range(3)]
-        if k == 0 or step == 0:
-            speeds = [cur[k, c, 3 + axis] for axis in range(3)]
-        else:
-            speeds = [halo_vel[step - 1, k - 1, c, axis] for axis in range(3)]
-            places = [p + TIME_STEP * v for p, v in zip(places, speeds)]
+    def kick_of(step, k, half):
+        if step == 0:
+            return cur[k, half.start // 8, 6]
+        if k == 0:
+            return kick_in[step, half]
+        return halo_kick[k, step - 1, half]
+
+    HALVES = (slice(0, 8), slice(8, 16))
+
+    def load(step, k):
+        for c, half in enumerate(HALVES):
+            if k in (1, 3) and step:
+                for axis in range(3):
+                    speed = halo_vel[step - 1, k // 2, c, axis]
+                    cur[k, c, 3 + axis] = speed
+                    cur[k, c, axis] += TIME_STEP * speed
+            tail = cur[k, c, 7]
+            push = KICK_SCALE * kick_of(step, k, half)
+            fields = [cur[k, c, axis] for axis in range(3)]
+            fields += [FRICTION * cur[k, c, 3 + axis] for axis in range(3)]
+            fields += [
+                push + (REPEL_SAME + (REPEL_CROSS - REPEL_SAME) * tail),
+                push + (REPEL_CROSS + (REPEL_SAME - REPEL_CROSS) * tail),
+            ]
+            for n, b in enumerate((-1, 0, 1)):
+                for f, field in enumerate(fields):
+                    if b:
+                        field = pltpu.roll(field, (-b) % NZ, 1)
+                    if f == 2:
+                        field = field + float(b)
+                    near[k, n, c, f] = field
+
+    PLACE = (0, 1, -1, -2)
+
+    def act(step, k, on, totals):
+        sides = [(t, c) for t in on for c in range(2)]
+        held = []
+        for t, c in sides:
+            apart = float(PLACE[k] - PLACE[t])
+            x = cur[t, c, 0]
+            held.append(
+                (
+                    x - apart * side if apart else x,
+                    cur[t, c, 1],
+                    cur[t, c, 2],
+                    FRICTION * cur[t, c, 3],
+                    FRICTION * cur[t, c, 4],
+                    FRICTION * cur[t, c, 5],
+                    KICK_SCALE * kick_of(step, t, HALVES[c]),
+                    cur[t, c, 7] > 0.5,
+                )
+            )
+
+        def tile(n, forces):
+            forces = list(forces)
+            for j in range(CAP):
+                xj, yj, zj, uj, vj, wj, a0, a1 = [
+                    near[k, n, j // 8, f, j % 8 : j % 8 + 1, :] for f in range(8)
+                ]
+                for i, (x, y, z, u, v, w, push, tail) in enumerate(held):
+                    dx = x - xj
+                    dy = y - yj
+                    dz = z - zj
+                    weight = jnp.maximum(1.0 - (dx * dx + dy * dy + dz * dz), 0.0)
+                    closing = dx * (u - uj) + dy * (v - vj) + dz * (w - wj)
+                    strength = weight * ((jnp.where(tail, a1, a0) + push) - weight * closing)
+                    fx, fy, fz = forces[i]
+                    forces[i] = (fx + strength * dx, fy + strength * dy, fz + strength * dz)
+            return tuple(forces)
+
+        forces = tuple(totals[side_] for side_ in sides)
+        for n in range(3):
+            forces = tile(n, forces)
+        for side_, force in zip(sides, forces):
+            totals[side_] = force
+
+    def bond(t, totals):
+        for c, half in enumerate(HALVES):
+            places = [cur[t, c, axis] for axis in range(3)]
+            found = list(places)
+            for j in range(CAP):
+                match = partners[t, half] == j
+                for axis in range(3):
+                    found[axis] = jnp.where(
+                        match, cur[t, j // 8, axis, j % 8 : j % 8 + 1, :], found[axis]
+                    )
+            totals[t, c] = tuple(-BOND_STIFF * (p - f) for p, f in zip(places, found))
+
+    def advance(step, t, totals, flow):
+        for c in range(2):
+            here = cur[t, c, 0] < 0.5 * FAR
+            for axis in range(3):
+                speed = cur[t, c, 3 + axis]
+                force = totals[t, c][axis] + (flow[axis : axis + 1] - DRAG_RATE * speed)
+                speed = jnp.where(here, speed + TIME_STEP * force, 0.0)
+                cur[t, c, 3 + axis] = speed
+                if t == 0 and step < STEPS - 1:
+                    vel_send[step, c, axis] = speed
+                if t == 0 and step == STEPS - 1:
+                    vel_out[axis, HALVES[c]] = speed
             if step < STEPS - 1:
                 for axis in range(3):
-                    cur[k, c, axis] = places[axis]
-        if step == 0:
-            kick = cur[k, c, 6]
-        elif k == 0:
-            kick = kick_in[step, half]
-        else:
-            kick = halo_kick[k - 1, step - 1, half]
-        tail = cur[k, c, 7]
-        push = KICK_SCALE * kick
-        fields = [
-            places[0] + shift,
-            places[1],
-            places[2],
-            FRICTION * speeds[0],
-            FRICTION * speeds[1],
-            FRICTION * speeds[2],
-            push + (REPEL_SAME + (REPEL_CROSS - REPEL_SAME) * tail),
-            push + (REPEL_CROSS + (REPEL_SAME - REPEL_CROSS) * tail),
-        ]
-        for n, b in enumerate((-1, 0, 1)):
-            for f, field in enumerate(fields):
-                if b:
-                    field = pltpu.roll(field, (-b) % NZ, 1)
-                if f == 2:
-                    field = field + float(b)
-                near[c, n, f] = field
-
-    def add_forces(step, c, own, totals):
-        half = slice(8 * own, 8 * own + 8)
-        xi, yi, zi = [cur[0, own, axis] for axis in range(3)]
-        ui, vi, wi = [FRICTION * cur[0, own, 3 + axis] for axis in range(3)]
-        ki = KICK_SCALE * kick_in[step, half]
-        tail = own_tail[half]
-        fx, fy, fz = totals
-        for n in range(3):
-            for j in range(8):
-                xj, yj, zj, uj, vj, wj, a0, a1 = [near[c, n, f, j : j + 1, :] for f in range(8)]
-                dx = xi - xj
-                dy = yi - yj
-                dz = zi - zj
-                weight = jnp.maximum(1.0 - (dx * dx + dy * dy + dz * dz), 0.0)
-                closing = dx * (ui - uj) + dy * (vi - vj) + dz * (wi - wj)
-                lift = jnp.where(tail, a1, a0) + ki
-                strength = weight * (lift - weight * closing)
-                fx = fx + strength * dx
-                fy = fy + strength * dy
-                fz = fz + strength * dz
-        return fx, fy, fz
-
-    loads["partner"].wait()
-    partner = partner_in[...]
-    partner = jnp.where(partner < count, partner, slot_ids)
-
-    def bond_forces(own):
-        places = [cur[0, own, axis] for axis in range(3)]
-        found = list(places)
-        for j in range(CAP):
-            match = partner[8 * own : 8 * own + 8] == j
-            for axis in range(3):
-                found[axis] = jnp.where(match, cur[0, j // 8, axis, j % 8 : j % 8 + 1, :], found[axis])
-        return tuple(-BOND_STIFF * (p - f) for p, f in zip(places, found))
+                    cur[t, c, axis] += TIME_STEP * cur[t, c, 3 + axis]
 
     def cell_copies():
         other = MIDDLE + 1 - mid
@@ -443,11 +479,6 @@
 
         @pl.when(is_mid)
         def _():
-            pl.semaphore_wait(sem_entered, 1)
-            for n in range(GROUPS):
-                pl.semaphore_signal(
-                    sem_ready, inc=1, device_id=(n, pair[1][1]), device_id_type=MESH
-                )
             for n, value in enumerate([density] + velocity + [row_ids.astype(F32)]):
                 cells[0, mid, n : n + 1, :] = jnp.sum(
                     jnp.where(at_cell, value, 0.0), axis=0, keepdims=True
@@ -457,69 +488,87 @@
 
         return copies
 
-    def advance(step, own, totals):
-        half = slice(8 * own, 8 * own + 8)
-        for axis in range(3):
-            speed = cur[0, own, 3 + axis]
-            force = totals[axis] + (flow[axis : axis + 1] - DRAG_RATE * speed)
-            speed = jnp.where(occupied[half], speed + TIME_STEP * force, 0.0)
-            cur[0, own, 3 + axis] = speed
-            if step < STEPS - 1:
-                vel_send[step, own, axis] = speed
+    def wait_drag(column):
+        for n in range(2):
+
+            def wait():
+                remote(
+                    drag.at[column, n],
+                    drag.at[column, n],
+                    sem_drag.at[0],
+                    sem_drag.at[31 + 2 * column + n],
+                    peers[0],
+                ).wait_recv()
+
+            if column:
+                wait()
             else:
-                vel_out[axis, half] = speed
-
-    def wait_drag():
-        for n in range(2):
-
-            @pl.when(me_g != MIDDLE + n)
-            def _():
-                remote(
-                    drag.at[n], drag.at[n], sem_drag.at[0], sem_drag.at[16 + n], peers[0]
-                ).wait_recv()
-
-        for copy in cur_copies:
-            copy.wait_send()
-        return (DRAG_RATE / VELOCITY_SCALE) * (drag[0, 0:3] + drag[1, 0:3])
-
-    for step in range(STEPS):
-        totals = [bond_forces(own) for own in range(2)]
-        for k in range(3):
-            if step == 0 and k == 2:
-                pl.semaphore_wait(sem_corner, 2)
-                post_copies = send_post(0)
-            if step == 1 and k == 2:
-                post_copies = lattice_between()
-            if k == 1:
-                near_copy.wait_recv()
-            if step == 1 and k:
-                kick_copies[k - 1].wait_recv()
-            for c in range(2):
-                if k == 2:
-                    far_copies[c].wait_recv()
-                load_near(step, k, c)
-                sent = []
-                for own in range(2):
-                    totals[own] = add_forces(step, c, own, totals[own])
-                    if k == 2 and c == 1:
-                        if step == 0 and own == 0:
-                            flow = wait_drag()
-                        advance(step, own, totals[own])
-                        if step < STEPS - 1:
-                            sent.append(
-                                send_far(
-                                    vel_send.at[step, own],
-                                    halo_vel.at[step, 1, own],
-                                    sem_vel.at[step],
-                                    own,
-                                )
-                            )
-        if step < STEPS - 1:
-            far_copies = sent
-            near_copy = send_near(vel_send.at[step], halo_vel.at[step, 0], sem_vel.at[step])
-            for own in range(2):
-                for axis in range(3):
-                    cur[0, own, axis] += TIME_STEP * cur[0, own, 3 + axis]
+                pl.when(me_g != MIDDLE + n)(wait)
+        return (DRAG_RATE / VELOCITY_SCALE) * (drag[column, 0, 0:3] + drag[column, 1, 0:3])
+
+    totals = {}
+    bond(0, totals)
+    load(0, 0)
+    act(0, 0, (0,), totals)
+    cur_copies[1].wait_recv()
+    load(0, 1)
+    act(0, 1, (0,), totals)
+    pl.semaphore_wait(sem_corner, 2)
+    post_copies = send_post(0)
+    cur_copies[2].wait_recv()
+    partner_copies[2].wait_recv()
+    bond(2, totals)
+    load(0, 2)
+    act(0, 2, (0, 2), totals)
+    flow = wait_drag(0)
+    for copy in cur_copies.values():
+        copy.wait_send()
+    advance(0, 0, totals, flow)
+    vel_copies = {
+        3: send(vel_send.at[0], halo_vel.at[0, 1], sem_vel.at[0, 2], sem_vel.at[1, 2], ahead2),
+        1: send(vel_send.at[0], halo_vel.at[0, 0], sem_vel.at[0, 0], sem_vel.at[1, 0], pair[0]),
+    }
+    act(0, 0, (2,), totals)
+    cur_copies[3].wait_recv()
+    load(0, 3)
+    act(0, 3, (2,), totals)
+
+    later = {}
+    for copy in kick_copies.values():
+        copy.wait_recv()
+    bond(0, later)
+    load(1, 0)
+    act(1, 0, (0,), later)
+    vel_copies[1].wait_recv()
+    load(1, 1)
+    act(1, 1, (0,), later)
+    post_copies = lattice_between()
+
+    far_flow = wait_drag(1)
+    advance(0, 2, totals, far_flow)
+    totals = later
+    bond(2, totals)
+    load(1, 2)
+    act(1, 2, (0, 2), totals)
+    advance(1, 0, totals, flow)
+    vel_copies[1] = send(
+        vel_send.at[1], halo_vel.at[1, 0], sem_vel.at[0, 1], sem_vel.at[1, 1], pair[0]
+    )
+    act(1, 0, (2,), totals)
+    vel_copies[3].wait_recv()
+    load(1, 3)
+    act(1, 3, (2,), totals)
+    advance(1, 2, totals, far_flow)
+
+    bond(0, totals)
+    load(2, 0)
+    act(2, 0, (0,), totals)
+    load(2, 2)
+    act(2, 2, (0,), totals)
+    vel_copies[1].wait_recv()
+    load(2, 1)
+    act(2, 1, (0,), totals)
+    advance(2, 0, totals, flow)
 
     for axis in range(3):
         sums[me_g, axis : axis + 1, :] = jnp.sum(
@@ -528,7 +577,6 @@
     sums[me_g, 3:4, :] = count.astype(F32)
     for k in FARTHEST:
         remote(sums.at[me_g], sums.at[me_g], sem_sum.at[0], sem_sum.at[1], peers[k - 1]).start()
-    pl.semaphore_wait(sem_ready, len(far_mids))
     for n in range(2):
         remote(
             sums.at[me_g], sums.at[GROUPS + me_g], sem_sum.at[0], sem_sum.at[2], far_mids[n]
@@ -539,8 +587,7 @@
         return remote(part, part, sem_sum.at[0], recv_sem, peers[0])
 
     for axis in range(3):
-        for own in range(2):
-            half = slice(8 * own, 8 * own + 8)
+        for own, half in enumerate(HALVES):
             place = cur[0, own, axis] + TIME_STEP * cur[0, own, 3 + axis]
             pos_out[axis, half] = jnp.where(occupied[half], place, 0.0)
     for copy in post_copies:
@@ -550,7 +597,7 @@
         pop_out[q] = g[q]
 
     for copy in unsent:
-        if not any(copy is other for other in cur_copies):
+        if not any(copy is other for other in cur_copies.values()):
             copy.wait_send()
 
     def pooled(which):
@@ -667,12 +714,13 @@
             pltpu.VMEM(bead, jnp.int32),
             pltpu.VMEM((1, NZ), jnp.int32),
             dma((8,)),
-            pltpu.VMEM((3, 2, 8, 8, NZ), F32),
-            pltpu.VMEM((2, 2, *bead), F32),
+            pltpu.VMEM((4, 2, 8, 8, NZ), F32),
+            pltpu.VMEM((3, *bead), jnp.int32),
+            pltpu.VMEM((4, 2, *bead), F32),
             pltpu.VMEM((2, 2, 3, 8, NZ), F32),
             pltpu.VMEM((2, 2, 2, 3, 8, NZ), F32),
-            pltpu.VMEM((2, 3, 8, 8, NZ), F32),
-            pltpu.VMEM((2, 4, NZ), F32),
+            pltpu.VMEM((4, 3, 2, 8, 8, NZ), F32),
+            pltpu.VMEM((2, 2, 4, NZ), F32),
             pltpu.VMEM((2, Q, LY, NZ), F32),
             pltpu.VMEM((2, 2, 5, LY, NZ), F32),
             pltpu.VMEM((2, 2, 5, LY, NZ), F32),
@@ -682,16 +730,15 @@
             pltpu.VMEM((2 * GROUPS, 4, NZ), F32),
             pltpu.VMEM((3, 8, NZ), F32),
             dma((2, 3)),
-            dma((2, 2)),
-            dma((2, 2, 3)),
-            dma((18,)),
+            dma((2, 3)),
+            dma((2, 3)),
+            dma((2, 3)),
+            dma((35,)),
             dma((2, 2, 2)),
             dma((2, 2, 2, 3)),
             dma((11,)),
             dma((3,)),
             dma((2,)),
-            pltpu.SemaphoreType.REGULAR,
-            pltpu.SemaphoreType.REGULAR,
             pltpu.SemaphoreType.REGULAR,
         ],
         compiler_params=pltpu.CompilerParams(

time: 35.3 us -> 33.8 us (0.958)
  the two profiles are of different devices: /device:TPU:33 before, /device:TPU:8 now
where the time goes in v6:
time: 33.8 us; the launch traced here: 33.7 us
  Pallas kernels  33 us (98%)
  between operations  0.64 us (2%)
    pallas_call x1, Pallas kernels, local(): pl.pallas_call(kernel, out_shape=(pltpu.VMEM((Q, LY, NZ), F32), pltpu.VME...  32.4 us
    pallas_call x1, Pallas kernels, local(): pl.pallas_call(hand_out, out_shape=tuple((jax.ShapeDtypeStruct(x.shape, F...  0.68 us

profile of v6, /device:TPU:8, one launch (start us, length us, event | category | flops | bytes accessed | tf_op | source)
XLA Modules:
  0.0 33.7 jit_solution(4273703647939021859)
XLA Ops:
  0.6 32.4 %cycle.1 = (f32[19,8,128]{2,1,0:T(8,128)S(1)}, f32[3,1,128]{2,1,0:T(1,128)S(1)}, f32[3,16,128]{2,1,0:T(8,128)S(1)}, f32[3,16,128]{2,1,0:T(8,128)S(1)}) custom-call(f32[19,8,128]{2,1,0:T(8,128)} %bitcast.16, s32[1,128]{1,0:T(1,128)} %rows_hbm.1, f32[3,16,128]{2,1,0:T(8,128)} %bitcast.17, f32[3,16,128]{2,1,0:T(8,128)} %bitcast.18, f32[3,16,128]{2,1,0:T(8,128)} %bitcast.19, ...), custom_call_target="tpu_custom_call" | custom-call | tf_op jit(solution)/shard_map/cycle/pallas_call | solution.py:697
  33.0 0.7 %hand_out.1 = (f32[19,8,128]{2,1,0:T(8,128)}, f32[3,1,128]{2,1,0:T(1,128)}, f32[3,16,128]{2,1,0:T(8,128)}, f32[3,16,128]{2,1,0:T(8,128)}) custom-call(f32[19,8,128]{2,1,0:T(8,128)S(1)} %get-tuple-element.12.refs_0_, f32[3,1,128]{2,1,0:T(1,128)S(1)} %get-tuple-element.13.refs_1_, f32[3,16,128]{2,1,0:T(8,128)S(1)} %get-tuple-element.14.refs_2_, ...), custom_call_target="tpu_custom_call" | custom-call | tf_op jit(solution)/shard_map/hand_out/pallas_call | solution.py:763

commit v7 on v6

--- a/solution.py
+++ b/solution.py
@@ -245,7 +245,7 @@
             for k in which
         }
 
-    cur_copies = spread(cur.at[0], cur, sem_cur, (2, 3, 1))
+    cur_copies = spread(cur.at[0], cur, sem_cur, (2, 1))
     partner_copies = spread(partners.at[0], partners, sem_partner, (2,))
 
     for group in (up_g, dn_g):
@@ -282,11 +282,6 @@
         for copy in drag_copies():
             copy.start()
 
-    kick_copies = spread(kick_in.at[pl.ds(1, 2)], halo_kick, sem_kick, (2, 1))
-    kick_copies[3] = send(
-        kick_in.at[1], halo_kick.at[3, 0], sem_kick.at[0, 2], sem_kick.at[1, 2], ahead2
-    )
-
     def store_post(stage, values):
         for q in range(Q):
             post[stage, q] = values[q]
@@ -298,6 +293,12 @@
                 row_send[stage, way, n] = values[q][edge : edge + 1, :]
 
     store_post(0, collide(g, density, inverse, velocity))
+
+    cur_copies.update(spread(cur.at[0], cur, sem_cur, (3,)))
+    kick_copies = spread(kick_in.at[pl.ds(1, 2)], halo_kick, sem_kick, (2, 1))
+    kick_copies[3] = send(
+        kick_in.at[1], halo_kick.at[3, 0], sem_kick.at[0, 2], sem_kick.at[1, 2], ahead2
+    )
 
     def send_post(stage):
         copies = []
@@ -555,32 +556,50 @@
         vel_send.at[1], halo_vel.at[1, 0], sem_vel.at[0, 1], sem_vel.at[1, 1], pair[0]
     )
     act(1, 0, (2,), totals)
-    vel_copies[3].wait_recv()
-    load(1, 3)
-    act(1, 3, (2,), totals)
-    advance(1, 2, totals, far_flow)
-
-    bond(0, totals)
+
+    later = {}
+    bond(0, later)
     load(2, 0)
-    act(2, 0, (0,), totals)
-    load(2, 2)
-    act(2, 2, (0,), totals)
-    vel_copies[1].wait_recv()
-    load(2, 1)
-    act(2, 1, (0,), totals)
-    advance(2, 0, totals, flow)
+    act(2, 0, (0,), later)
+    def with_near(forces):
+        found = {(0, c): forces[c] for c in range(2)}
+        vel_copies[1].wait_recv()
+        load(2, 1)
+        act(2, 1, (0,), found)
+        return found[0, 0], found[0, 1]
+
+    def with_far(forces):
+        found = {(0, c): forces[c] for c in range(2)}
+        far_totals = {(2, c): totals[2, c] for c in range(2)}
+        vel_copies[3].wait_recv()
+        load(1, 3)
+        act(1, 3, (2,), far_totals)
+        advance(1, 2, far_totals, far_flow)
+        load(2, 2)
+        act(2, 2, (0,), found)
+        return found[0, 0], found[0, 1]
+
+    slow_far = lax.rem((me_b + 1) // 2, 2) == 0
+    forces = lax.fori_loop(
+        0,
+        2,
+        lambda turn, forces: lax.cond((turn == 0) == slow_far, with_near, with_far, forces),
+        (later[0, 0], later[0, 1]),
+    )
+    later = {(0, c): forces[c] for c in range(2)}
+    advance(2, 0, later, flow)
 
     for axis in range(3):
         sums[me_g, axis : axis + 1, :] = jnp.sum(
             cur[0, 0, 3 + axis] + cur[0, 1, 3 + axis], axis=0, keepdims=True
         )
     sums[me_g, 3:4, :] = count.astype(F32)
-    for k in FARTHEST:
-        remote(sums.at[me_g], sums.at[me_g], sem_sum.at[0], sem_sum.at[1], peers[k - 1]).start()
     for n in range(2):
         remote(
             sums.at[me_g], sums.at[GROUPS + me_g], sem_sum.at[0], sem_sum.at[2], far_mids[n]
         ).start()
+    for k in FARTHEST:
+        remote(sums.at[me_g], sums.at[me_g], sem_sum.at[0], sem_sum.at[1], peers[k - 1]).start()
 
     def all_sums(start, size, recv_sem):
         part = sums.at[pl.ds(start, size)]

time: 33.8 us -> 33.6 us (level)
  the two profiles are of different devices: /device:TPU:8 before, /device:TPU:88 now
where the time goes in v7:
time: 33.6 us; the launch traced here: 33.5 us
  Pallas kernels  32.8 us (98%)
  between operations  0.64 us (2%)
    pallas_call x1, Pallas kernels, local(): pl.pallas_call(kernel, out_shape=(pltpu.VMEM((Q, LY, NZ), F32), pltpu.VME...  32.2 us
    pallas_call x1, Pallas kernels, local(): pl.pallas_call(hand_out, out_shape=tuple((jax.ShapeDtypeStruct(x.shape, F...  0.68 us

profile of v7, /device:TPU:88, one launch (start us, length us, event | category | flops | bytes accessed | tf_op | source)
XLA Modules:
  0.0 33.5 jit_solution(10103329107074652169)
XLA Ops:
  0.6 32.2 %cycle.1 = (f32[19,8,128]{2,1,0:T(8,128)S(1)}, f32[3,1,128]{2,1,0:T(1,128)S(1)}, f32[3,16,128]{2,1,0:T(8,128)S(1)}, f32[3,16,128]{2,1,0:T(8,128)S(1)}) custom-call(f32[19,8,128]{2,1,0:T(8,128)} %bitcast.16, s32[1,128]{1,0:T(1,128)} %rows_hbm.1, f32[3,16,128]{2,1,0:T(8,128)} %bitcast.17, f32[3,16,128]{2,1,0:T(8,128)} %bitcast.18, f32[3,16,128]{2,1,0:T(8,128)} %bitcast.19, ...), custom_call_target="tpu_custom_call" | custom-call | tf_op jit(solution)/shard_map/cycle/pallas_call | solution.py:716
  32.8 0.7 %hand_out.1 = (f32[19,8,128]{2,1,0:T(8,128)}, f32[3,1,128]{2,1,0:T(1,128)}, f32[3,16,128]{2,1,0:T(8,128)}, f32[3,16,128]{2,1,0:T(8,128)}) custom-call(f32[19,8,128]{2,1,0:T(8,128)S(1)} %get-tuple-element.12.refs_0_, f32[3,1,128]{2,1,0:T(1,128)S(1)} %get-tuple-element.13.refs_1_, f32[3,16,128]{2,1,0:T(8,128)S(1)} %get-tuple-element.14.refs_2_, ...), custom_call_target="tpu_custom_call" | custom-call | tf_op jit(solution)/shard_map/hand_out/pallas_call | solution.py:782
